TPU v7x, 256 devices: a whole 4x4x8 slice. The times are simulated.
256 devices in a mesh: seq: 2 (over y_lo), row: 16 (over z, core), col: 8 (over x, y_hi).
Axes of the slice: x: 4, y: 4 (y_hi: 2, y_lo: 2; y = y_hi * 2 + y_lo), z: 8, core: 2. Of those that a mesh axis runs over, the one named last changes fastest.
Arguments:
- hidden: bfloat16 [4096, 5120], P('seq', 'row'), may hold values from -6 to 6
- w_query: bfloat16 [5120, 4096], P('row', 'col'), may hold values from -0.5031153 to 0.5031153
- w_key: bfloat16 [5120, 1024], P('row', 'col'), may hold values from -0.5031153 to 0.5031153
- w_value: bfloat16 [5120, 1024], P('row', 'col'), may hold values from -0.078125 to 0.078125
- w_ssm_in: bfloat16 [5120, 4096], P('row', 'col'), may hold values from -0.078125 to 0.078125
- w_gate: bfloat16 [5120, 4096], P('row', 'col'), may hold values from -0.078125 to 0.078125
- w_bc: bfloat16 [5120, 256], P('row'), may hold values from -0.078125 to 0.078125
- w_dt: bfloat16 [5120, 64], P('row', 'col'), may hold values from -0.078125 to 0.078125
- dt_bias: float32 [64], P('col'), may hold values from -2 to 0.5
- a_rate: float32 [64], P('col'), may hold values from 0.00012207031 to 0.04
- d_skip: float32 [64], P('col'), may hold values from 0.5 to 1.5
- w_attn_out: bfloat16 [4096, 5120], P('col', 'row'), may hold values from -0.09375 to 0.09375
- w_ssm_out: bfloat16 [4096, 5120], P('col', 'row'), may hold values from -0.09375 to 0.09375
Outputs:
- mixed: bfloat16 [4096, 5120], P(('seq', 'col'), 'row')
All inputs are finite; a program needn't handle non-finite values.
Results may differ from a plain program's by a relative error of at most 0.017.
The roundings to bfloat16 on the way count: a program that leaves them out, or rounds other values in their place, can miss the bound.
Values may be sent and summed in bfloat16 or wider, within the bound.
No kernel may reach another device: no remote copies, remote signals or barrier semaphores. Data moves between devices by JAX's collectives and lax.ppermute only.
A program may use at most 128 MiB of HBM per device.

v0:
```python
import jax
import jax.numpy as jnp
from jax import lax
from jax.sharding import PartitionSpec as P

HD = 128


def carried_in(array, axis, join, neutral):
    place = lax.axis_index(axis)
    gathered = jax.tree.map(
        lambda a, kind: lax.all_gather(a.astype(kind), axis), array, (jnp.bfloat16, jnp.bfloat16)
    )
    state = jax.tree.map(lambda a, e: jnp.zeros_like(a) + jnp.asarray(e, a.dtype), array, neutral)

    def one(lap, state):
        return join(
            state,
            jax.tree.map(
                lambda a, own: lax.dynamic_index_in_dim(a, lap, 0, False).astype(own.dtype),
                gathered,
                array,
            ),
        )

    return lax.fori_loop(0, place, one, state)


def attention_block(query, keys, values):
    tok_rows = query.shape[0]
    head_count = query.shape[1] // HD
    kv_heads = keys.shape[1] // HD
    group = head_count // kv_heads
    grouped = query.reshape(tok_rows, kv_heads, group, HD)
    anchor = lax.axis_index(("seq", "row")) * tok_rows
    query_pos = anchor + jnp.arange(tok_rows, dtype=jnp.int32)
    scale = HD ** (-0.5)
    best = jnp.full((kv_heads, group, tok_rows), -1e30, jnp.float32)
    key_piece = lax.all_gather(keys, ("seq", "row"), axis=0, tiled=True)
    value_piece = lax.all_gather(values, ("seq", "row"), axis=0, tiled=True)
    length = key_piece.shape[0]
    key_pos = jnp.arange(length, dtype=jnp.int32)
    scores = (
        jnp.einsum(
            "tkgd,mkd->kgtm",
            grouped,
            key_piece.reshape(length, kv_heads, HD),
            preferred_element_type=jnp.float32,
        )
        * scale
    )
    valid = jnp.logical_and(key_pos[None, :] <= query_pos[:, None], key_pos[None, :] >= 0)
    scores = jnp.where(valid, scores, -1e30)
    new_best = jnp.maximum(best, jnp.max(scores, axis=-1))
    weights = jnp.where(valid, jnp.exp(scores - new_best[..., None]), 0.0)
    total = jnp.sum(weights, axis=-1)
    value_float = value_piece.reshape(length, kv_heads, HD).astype(jnp.float32)
    summed = jnp.einsum("kgtm,mkd->kgtd", weights, value_float, precision=lax.Precision.HIGHEST)
    best, total, summed = (new_best, total, summed)
    output = summed / total[..., None]
    return output.transpose(2, 0, 1, 3).reshape(tok_rows, head_count * HD).astype(jnp.bfloat16)


def ssd_block(ssm_raw, gate_raw, bc_raw, dt_raw, dt_bias, a_rate, d_skip):
    highest = lax.Precision.HIGHEST
    tok_rows = ssm_raw.shape[0]
    heads = dt_raw.shape[1]
    head_size = ssm_raw.shape[1] // heads
    state_size = bc_raw.shape[1] // 2
    inputs = jax.nn.silu(ssm_raw).reshape(tok_rows, heads, head_size)
    gates = gate_raw.reshape(tok_rows, heads, head_size)
    bc_act = jax.nn.silu(bc_raw)
    b_rows = bc_act[:, :state_size]
    c_rows = bc_act[:, state_size:]
    step_size = jax.nn.softplus(dt_raw + dt_bias[None, :])
    cumulative = jnp.cumsum(-a_rate[None, :] * step_size, axis=0)
    position = jnp.arange(tok_rows)
    lower = position[:, None] >= position[None, :]
    inner = jnp.dot(c_rows, b_rows.T, precision=highest)
    decays = jnp.exp(
        jnp.where(lower[:, :, None], cumulative[:, None, :] - cumulative[None, :, :], -jnp.inf)
    )
    coefficient = inner[:, :, None] * decays * step_size[None, :, :]
    within = jnp.einsum("tuh,uhp->thp", coefficient, inputs, precision=highest)
    to_end = jnp.exp(cumulative[-1][None, :] - cumulative) * step_size
    local_state = jnp.einsum("uh,uhp,un->hpn", to_end, inputs, b_rows, precision=highest)
    block_decay = jnp.exp(cumulative[-1])

    def chain(earlier, later):
        return (earlier[0] * later[0], later[0][:, None, None] * earlier[1] + later[1])

    identity = (jnp.ones_like(block_decay), jnp.zeros_like(local_state))
    prior_decay, prior_state = carried_in(
        (block_decay, local_state), ("seq", "row"), chain, identity
    )
    carried = jnp.exp(cumulative)[:, :, None] * jnp.einsum(
        "hpn,tn->thp", prior_state, c_rows, precision=highest
    )
    result = within + carried + d_skip[None, :, None] * inputs
    gated = result * jax.nn.silu(gates)
    normed = gated * lax.rsqrt(jnp.mean(gated * gated, axis=-1, keepdims=True) + 1e-05)
    return normed.reshape(tok_rows, heads * head_size).astype(jnp.bfloat16)


def on_device(
    hidden,
    w_query,
    w_key,
    w_value,
    w_ssm_in,
    w_gate,
    w_bc,
    w_dt,
    dt_bias,
    a_rate,
    d_skip,
    w_attn_out,
    w_ssm_out,
):
    own_tokens = lax.all_to_all(hidden, "row", split_axis=0, concat_axis=1, tiled=True)
    pieces = (
        lax.all_gather(w_query, "row", axis=0, tiled=True),
        lax.all_gather(w_key, "row", axis=0, tiled=True),
        lax.all_gather(w_value, "row", axis=0, tiled=True),
        lax.all_gather(w_ssm_in, "row", axis=0, tiled=True),
        lax.all_gather(w_gate, "row", axis=0, tiled=True),
        lax.all_gather(w_bc, "row", axis=0, tiled=True),
        lax.all_gather(w_dt, "row", axis=0, tiled=True),
    )
    parts = tuple(
        (jnp.dot(own_tokens, piece, preferred_element_type=jnp.float32) for piece in pieces)
    )
    query_raw, key_raw, value_raw, ssm_raw, gate_raw, bc_raw, dt_raw = parts
    attn_out = attention_block(
        query_raw.astype(jnp.bfloat16), key_raw.astype(jnp.bfloat16), value_raw.astype(jnp.bfloat16)
    )
    ssm_out = ssd_block(ssm_raw, gate_raw, bc_raw, dt_raw, dt_bias, a_rate, d_skip)
    mixer = jnp.concatenate([attn_out, ssm_out], axis=1)
    attn_width = attn_out.shape[1]
    piece = lax.all_gather(mixer, "row", axis=0, tiled=True)
    first = jnp.dot(piece[:, :attn_width], w_attn_out, preferred_element_type=jnp.float32)
    terms = first + jnp.dot(piece[:, attn_width:], w_ssm_out, preferred_element_type=jnp.float32)
    return lax.psum_scatter(terms.astype(jnp.bfloat16), "col", scatter_dimension=0, tiled=True)


def solution(mesh):
    in_specs = (
        P("seq", "row"),
        P("row", "col"),
        P("row", "col"),
        P("row", "col"),
        P("row", "col"),
        P("row", "col"),
        P("row", None),
        P("row", "col"),
        P("col"),
        P("col"),
        P("col"),
        P("col", "row"),
        P("col", "row"),
    )
    out_specs = P(("seq", "col"), "row")
    return jax.shard_map(
        on_device, mesh=mesh, in_specs=in_specs, out_specs=out_specs, check_vma=False
    )
```

profile of v0, /device:TPU:1, one launch (start us, length us, event | category | flops | bytes accessed | tf_op | source)
XLA Modules:
  0.0 635.5 jit_solution(10076399778147517024)
XLA Ops:
  10.9 50.1 %all_to_all.19 = bf16[16,128,320]{1,2,0:T(8,128)(2,1)S(1)} all-to-all(bf16[16,128,320]{1,2,0:T(8,128)(2,1)S(1)} %copy_bitcast_fusion), channel_id=1, replica_groups=mesh['seq'=2,'row'=16,'col'=8] {'row'}, dimensions={0} | all-to-all | bytes 2621440 | tf_op jit(solution)/shard_map/all_to_all | solution.py:120
  61.0 2.5 convolution_convert_fusion.3
  63.6 35.4 %all-gather.20.cloned.1.call-done = bf16[5120,128]{1,0:T(8,128)(2,1)} async-done(((bf16[320,128]{1,0:T(8,128)(2,1)}), bf16[5120,128]{1,0:T(8,128)(2,1)}) %all-gather.20.cloned.1.call-update) | async-done | bytes 1310736 | tf_op jit(solution)/shard_map/all_gather | solution.py:124
  99.0 2.5 convolution_convert_fusion.2
  101.5 15.9 %all-gather.1 = bf16[16,320,8]{1,2,0:T(8,128)(2,1)S(1)} all-gather(bf16[1,320,8]{1,2,0:T(8,128)(2,1)S(1)} %bitcast.124), channel_id=1, replica_groups=mesh['seq'=2,'row'=16,'col'=8] {'row'}, dimensions={0}, use_global_device_ids=true | all-gather | bytes 87040 | tf_op jit(solution)/shard_map/all_gather | solution.py:128
  118.3 21.6 %all-gather.26.cloned.1.call-done = bf16[5120,256]{1,0:T(8,128)(2,1)} async-done(((bf16[320,256]{1,0:T(8,128)(2,1)}), bf16[5120,256]{1,0:T(8,128)(2,1)}) %all-gather.26.cloned.1.call-update) | async-done | bytes 2621456 | tf_op jit(solution)/shard_map/all_gather | solution.py:127
  139.9 2.3 divide_multiply_fusion.1
  142.3 41.2 %all-gather.24.cloned.1.call-done = bf16[5120,512]{1,0:T(8,128)(2,1)} async-done(((bf16[320,512]{1,0:T(8,128)(2,1)}), bf16[5120,512]{1,0:T(8,128)(2,1)}) %all-gather.24.cloned.1.call-update) | async-done | bytes 5242896 | tf_op jit(solution)/shard_map/all_gather | solution.py:125
  183.5 3.4 divide_multiply_fusion
  187.1 1.0 convolution_convert_fusion
  189.2 1.5 exp.41
  190.6 33.6 %all-gather.2 = bf16[32,1,8]{2,1,0:T(2,128)(2,1)S(1)} all-gather(bf16[1,1,8]{2,1,0:T(2,128)(2,1)S(1)} %get-tuple-element.76), channel_id=1, replica_groups=mesh['seq'=2,'row'=16,'col'=8] {'seq','row'}, dimensions={0}, use_global_device_ids=true | all-gather | bytes 528 | tf_op jit(solution)/shard_map/all_gather | solution.py:12
  224.2 1.5 copy.63
  225.7 0.9 fusion.44
  226.6 0.8 all-gather.28.cloned.1.call-done
  227.5 8.0 %copy.67 = bf16[512,5120]{1,0:T(8,128)(2,1)} copy(bf16[512,5120]{0,1:T(8,128)(2,1)} %bitcast.116) | data formatting | bytes 10485760 | tf_op jit(solution)/shard_map/dot_general | solution.py:131
  235.4 35.5 %all-gather.18.cloned.1.call-done = bf16[5120,512]{1,0:T(8,128)(2,1)} async-done(((bf16[320,512]{1,0:T(8,128)(2,1)}), bf16[5120,512]{1,0:T(8,128)(2,1)}) %all-gather.18.cloned.1.call-update) | async-done | bytes 5242896 | tf_op jit(solution)/shard_map/all_gather | solution.py:122
  270.9 4.0 fusion.16
  275.0 60.1 %all-gather.16.cloned.1.call-done = bf16[4096,128]{1,0:T(8,128)(2,1)} async-done(((bf16[128,128]{1,0:T(8,128)(2,1)}), bf16[4096,128]{1,0:T(8,128)(2,1)}) %all-gather.16.cloned.1.call-update) | async-done | bytes 1048592 | tf_op jit(solution)/shard_map/all_gather | solution.py:39
  335.0 2.6 fusion.2
  337.7 2.5 convolution_bitcast_fusion
  340.2 2.2 fusion.52
  342.5 2.1 fusion.3
  344.5 55.7 %all-gather.22.cloned.1.call-done = bf16[4096,128]{1,0:T(8,128)(2,1)} async-done(((bf16[128,128]{1,0:T(8,128)(2,1)}), bf16[4096,128]{1,0:T(8,128)(2,1)}) %all-gather.22.cloned.1.call-update) | async-done | bytes 1048592 | tf_op jit(solution)/shard_map/all_gather | solution.py:40
  400.2 8.5 %fusion.20 = bf16[4,128,128]{1,2,0:T(8,128)(2,1)S(1)} fusion(f32[4096,128,4]{1,0,2:T(8,128)} %copy-done.2, f32[4,128]{1,0:T(4,128)} %copy-done.10, pred[128,4096]{0,1:T(8,128)(4,1)S(1)} %iota_compare_fusion, bf16[4096,128]{1,0:T(8,128)(2,1)} %all-gather.22.cloned.1.call-done, f32[4,128]{1,0:T(4,128)S(1)} %fusion.3), kind=kOutput, calls=%fused_computation.32 | convolution fusion | flops 3229745152 | bytes 10096640 | tf_op jit(solution)/shard_map/kgtm,mkd->kgtd/dot_general | solution.py:58
  408.7 59.9 %all-gather.32.cloned.1.call-done = bf16[256,64,128]{2,1,0:T(8,128)(2,1)} async-done(((bf16[8,64,128]{2,1,0:T(8,128)(2,1)}), bf16[256,64,128]{2,1,0:T(8,128)(2,1)}) %all-gather.32.cloned.1.call-update) | async-done | bytes 4194320 | tf_op jit(solution)/shard_map/all_gather | solution.py:12
  468.6 1.1 while.12
  468.7 1.1 convert_add_fusion.2
  471.1 77.4 %all-gather.30.cloned.1.call-done = bf16[2048,1024]{0,1:T(8,128)(2,1)} async-done(((bf16[128,1024]{0,1:T(8,128)(2,1)}), bf16[2048,1024]{0,1:T(8,128)(2,1)}) %all-gather.30.cloned.1.call-update) | async-done | bytes 4194320 | tf_op jit(solution)/shard_map/all_gather | solution.py:140
  548.5 2.6 fusion.11
  551.3 1.9 fusion.9
  553.3 75.7 %reduce-scatter.2.cloned.1.call-done = bf16[256,320]{0,1:T(8,128)(2,1)} async-done(((bf16[2048,320]{0,1:T(8,128)(2,1)}), bf16[256,320]{0,1:T(8,128)(2,1)}) %reduce-scatter.2.cloned.1.call-update) | async-done | bytes 163856 | tf_op jit(solution)/shard_map/reduce_scatter | solution.py:143
  (79 shorter events, 7.9 us)
Async XLA Ops:
  6.5 4.0 copy-start
  6.5 54.4 %all-gather.14.cloned.1.call-start = ((), (), s32[]{:S(2)}) async-start(), calls=%async_computation.2 | async-start | bytes 1392640 | tf_op jit(solution)/shard_map/all_gather | solution.py:123
  7.3 91.7 %all-gather.20.cloned.1.call-start = ((), (), s32[]{:S(2)}) async-start(), calls=%async_computation.5 | async-start | bytes 1392640 | tf_op jit(solution)/shard_map/all_gather | solution.py:124
  8.0 131.9 %all-gather.26.cloned.1.call-start = ((), (), s32[]{:S(2)}) async-start(), calls=%async_computation.8 | async-start | bytes 2785280 | tf_op jit(solution)/shard_map/all_gather | solution.py:127
  8.7 174.8 %all-gather.24.cloned.1.call-start = ((), (), s32[]{:S(2)}) async-start(), calls=%async_computation.7 | async-start | bytes 5570560 | tf_op jit(solution)/shard_map/all_gather | solution.py:125
  9.3 218.1 %all-gather.28.cloned.1.call-start = ((), (), s32[]{:S(2)}) async-start(), calls=%async_computation.9 | async-start | bytes 5570560 | tf_op jit(solution)/shard_map/all_gather | solution.py:126
  9.9 261.0 %all-gather.18.cloned.1.call-start = ((), (), s32[]{:S(2)}) async-start(), calls=%async_computation.4 | async-start | bytes 5570560 | tf_op jit(solution)/shard_map/all_gather | solution.py:122
  10.5 324.5 %all-gather.16.cloned.1.call-start = ((), (), s32[]{:S(2)}) async-start(), calls=%async_computation.3 | async-start | bytes 1081344 | tf_op jit(solution)/shard_map/all_gather | solution.py:39
  61.0 40.5 %copy-start.14 = (f32[8]{0:T(128)S(1)}, f32[8]{0:T(128)}, u32[]{:S(2)}) copy-start(f32[8]{0:T(128)} %param.24) | copy-start | bytes 100
  61.0 40.6 %copy-start.11 = (bf16[320,8]{0,1:T(8,128)(2,1)S(1)}, bf16[320,8]{0,1:T(8,128)(2,1)}, u32[]{:S(2)}) copy-start(bf16[320,8]{0,1:T(8,128)(2,1)} %param.22) | copy-start | bytes 15364
  61.0 56.6 %copy-start.13 = (f32[8]{0:T(128)S(1)}, f32[8]{0:T(128)}, u32[]{:S(2)}) copy-start(f32[8]{0:T(128)} %param.23) | copy-start | bytes 100
  63.5 336.7 %all-gather.22.cloned.1.call-start = ((), (), s32[]{:S(2)}) async-start(), calls=%async_computation.6 | async-start | bytes 1081344 | tf_op jit(solution)/shard_map/all_gather | solution.py:40
  101.5 367.2 %all-gather.32.cloned.1.call-start = ((), (), s32[]{:S(2)}) async-start(), calls=%async_computation.12 | async-start | bytes 4325376 | tf_op jit(solution)/shard_map/all_gather | solution.py:12
  118.2 24.1 %copy-start.6 = (f32[128,8]{1,0:T(8,128)}, f32[128,8]{1,0:T(8,128)S(1)}, u32[]{:S(2)}) copy-start(f32[128,8]{1,0:T(8,128)S(1)} %reduce_window_sum.11) | copy-start | bytes 12292
  188.1 360.3 %all-gather.30.cloned.1.call-start = ((), (), s32[]{:S(2)}) async-start(), calls=%async_computation.10 | async-start | bytes 4456448 | tf_op jit(solution)/shard_map/all_gather | solution.py:140
  335.0 2.7 copy-start.8
  335.0 2.7 copy-start.9
  335.0 5.2 copy-start.1
  337.7 4.8 copy-start.2
  337.7 4.8 copy-start.10
  408.7 61.1 %copy-start.5 = (f32[128,8,64]{0,2,1:T(8,128)S(1)}, f32[128,8,64]{0,2,1:T(8,128)}, u32[]{:S(2)}) copy-start(f32[128,8,64]{0,2,1:T(8,128)} %fusion.52) | copy-start | bytes 786436
  408.7 61.1 %copy-start.12 = (f32[128,8]{0,1:T(8,128)S(1)}, f32[128,8]{0,1:T(8,128)}, u32[]{:S(2)}) copy-start(f32[128,8]{0,1:T(8,128)} %copy.63) | copy-start | bytes 12292
  408.7 61.1 %copy-start.15 = (f32[8]{0:T(128)S(1)}, f32[8]{0:T(128)}, u32[]{:S(2)}) copy-start(f32[8]{0:T(128)} %param.25) | copy-start | bytes 100
  408.7 61.1 %copy-start.16 = (f32[128,8,64]{0,2,1:T(8,128)S(1)}, f32[128,8,64]{0,2,1:T(8,128)}, u32[]{:S(2)}) copy-start(f32[128,8,64]{0,2,1:T(8,128)} %convolution_bitcast_fusion) | copy-start | bytes 786436
  468.6 79.8 %copy-start.4 = (bf16[512,320]{0,1:T(8,128)(2,1)S(1)}, bf16[512,320]{0,1:T(8,128)(2,1)}, u32[]{:S(2)}) copy-start(bf16[512,320]{0,1:T(8,128)(2,1)} %param.26) | copy-start | bytes 983044
  471.1 80.0 %copy-start.7 = (bf16[512,320]{0,1:T(8,128)(2,1)S(1)}, bf16[512,320]{0,1:T(8,128)(2,1)}, u32[]{:S(2)}) copy-start(bf16[512,320]{0,1:T(8,128)(2,1)} %param.27) | copy-start | bytes 983044
  471.1 157.9 %reduce-scatter.2.cloned.1.call-start = ((), (), s32[]{:S(2)}) async-start(), calls=%async_computation.11 | async-start | bytes 1474560 | tf_op jit(solution)/shard_map/reduce_scatter | solution.py:143
  548.5 2.8 copy-start.3
Sparse Core Ops, SparseCore 0:
  9.2 48.6 all-gather.13
  59.7 39.1 all-gather.19
  100.8 39.0 all-gather.25
  141.6 41.8 all-gather.23
  185.2 42.1 all-gather.27
  229.1 41.7 all-gather.17
  272.8 62.1 all-gather.15
  336.9 63.2 all-gather.21
  402.1 66.5 all-gather.31
  471.2 77.2 all-gather.29
  553.4 75.5 reduce-scatter.1
where the time goes:
time: 637 us; the launch traced here: 635 us
  waiting for transfers between devices  467 us (73%)
  blocking collectives  99.6 us (16%)
  matrix products  37.8 us (6%)
  between operations  13.6 us (2%)
  local copies, waits for them, and re-layouts  12 us (2%)
    all_gather x1, waiting for transfers between devices, on_device(): piece = lax.all_gather(mixer, 'row', axis=0, tiled=True)  77.4 us
    reduce_scatter x1, waiting for transfers between devices, on_device(): lax.psum_scatter(terms.astype(jnp.bfloat16), 'col', scatter_dimension=0,...  75.7 us
    all_gather x1, waiting for transfers between devices, attention_block(): key_piece = lax.all_gather(keys, ('seq', 'row'), axis=0, tiled=True)  60.1 us
    all_gather x1, waiting for transfers between devices, carried_in(): lax.all_gather(a.astype(kind), axis)  59.9 us
    all_gather x1, waiting for transfers between devices, attention_block(): value_piece = lax.all_gather(values, ('seq', 'row'), axis=0, tiled=True)  55.7 us
    all_to_all x1, blocking collectives, on_device(): lax.all_to_all(hidden, 'row', split_axis=0, concat_axis=1, tiled=True)  50.1 us
    all_gather x1, waiting for transfers between devices, on_device(): lax.all_gather(w_ssm_in, 'row', axis=0, tiled=True)  41.2 us
    all_gather x1, waiting for transfers between devices, on_device(): lax.all_gather(w_query, 'row', axis=0, tiled=True)  35.5 us
  transfers between devices with their start and end apart: 11, of which 10 were waited for; matrix products, arithmetic and copies ran while one was open for 8% of the time, Pallas kernels for 0%

commit v1 on v0

v1 whole, which is shorter than its diff:
```python
import jax
import jax.numpy as jnp
from jax import lax
from jax.sharding import PartitionSpec as P

HD = 128
HP = 64
NSTATE = 128
RING = 8
ROWS = 16
COLS = 8
F32 = jnp.float32
BF16 = jnp.bfloat16
HIGHEST = lax.Precision.HIGHEST


def ring_step(array, step):
    return lax.ppermute(array, "row", [(i, (i + 2 * step) % ROWS) for i in range(ROWS)])


def other_core(array):
    return lax.ppermute(array, "row", [(i, i ^ 1) for i in range(ROWS)])


def ring_reduce(partial, wire, right_hops):
    left_hops = RING - 1 - right_hops
    right = left = None
    for hop in range(max(right_hops, left_hops), 0, -1):
        if hop <= right_hops:
            term = partial(hop)
            right = ring_step((term if right is None else right.astype(F32) + term).astype(wire), 1)
        if hop <= left_hops:
            term = partial(-hop)
            left = ring_step((term if left is None else left.astype(F32) + term).astype(wire), -1)
    return partial(0) + right.astype(F32) + left.astype(F32)


def attention(query, query_start, keys, values, key_start):
    tok_rows = query.shape[1]
    group = query.shape[0] // HD
    query_pos = query_start + jnp.arange(tok_rows, dtype=jnp.int32)
    key_pos = (key_start[:, None] + jnp.arange(tok_rows, dtype=jnp.int32)[None, :]).reshape(-1)
    grouped = query.reshape(group, HD, tok_rows)
    scores = jnp.einsum("gdt,dm->gtm", grouped, keys, preferred_element_type=F32) * HD ** (-0.5)
    valid = key_pos[None, :] <= query_pos[:, None]
    scores = jnp.where(valid, scores, -1e30)
    best = jnp.max(scores, axis=-1, keepdims=True)
    weights = jnp.exp(scores - best).astype(BF16)
    total = jnp.sum(weights.astype(F32), axis=-1)
    summed = jnp.einsum("gtm,md->gtd", weights, values, preferred_element_type=F32)
    output = summed / total[..., None]
    return output.transpose(1, 0, 2).reshape(tok_rows, group * HD).astype(BF16)


def on_device(
    hidden,
    w_query,
    w_key,
    w_value,
    w_ssm_in,
    w_gate,
    w_bc,
    w_dt,
    dt_bias,
    a_rate,
    d_skip,
    w_attn_out,
    w_ssm_out,
):
    row = lax.axis_index("row")
    seq = lax.axis_index("seq")
    chip = row // 2
    core = row % 2
    half_rows = hidden.shape[0]
    tok_rows = half_rows // ROWS
    heads = w_dt.shape[1]
    head_rows = heads * HP
    query_width = w_query.shape[1]
    kv_width = w_value.shape[1]
    bc_width = w_bc.shape[1]
    ssm_width = w_ssm_in.shape[1]

    hidden_other = other_core(hidden)
    w_wide = jnp.concatenate([w_query, w_key, w_bc, w_dt], axis=1)
    w_narrow = jnp.concatenate([w_value, w_ssm_in, w_gate], axis=1)
    w_wide, w_narrow = (jnp.concatenate([w, other_core(w)], axis=0) for w in (w_wide, w_narrow))

    def block_of(hop):
        start = (((chip + hop + RING) % RING) * 2 + core) * tok_rows
        return jnp.concatenate(
            [lax.dynamic_slice_in_dim(h, start, tok_rows, 0) for h in (hidden, hidden_other)], axis=1
        )

    blocks = {hop: block_of(hop) for hop in range(1 - RING // 2, RING // 2 + 1)}
    blocks[-RING // 2] = blocks[RING // 2]

    def project_wide(hop):
        return lax.dot_general(w_wide, blocks[hop], (((0,), (1,)), ((), ())), preferred_element_type=F32)

    def project_narrow(hop):
        return jnp.dot(blocks[hop], w_narrow, preferred_element_type=F32)

    narrow = ring_reduce(project_narrow, BF16, 3)
    wide = ring_reduce(project_wide, F32, 4)

    query = wide[:query_width].astype(BF16)
    key = wide[query_width : query_width + kv_width].astype(BF16)
    bc_act = jax.nn.silu(wide[query_width + kv_width : query_width + kv_width + bc_width])
    dt_raw = wide[query_width + kv_width + bc_width :]
    value = narrow[:, :kv_width].astype(BF16)
    inputs = jax.nn.silu(narrow[:, kv_width : kv_width + ssm_width])
    gate_raw = narrow[:, kv_width + ssm_width :]

    b_cols = bc_act[:NSTATE]
    c_cols = bc_act[NSTATE:]
    step_size = jax.nn.softplus(dt_raw + dt_bias[:, None])
    position = jnp.arange(tok_rows)
    upto = (position[:, None] <= position[None, :]).astype(F32)
    cumulative = jnp.dot(-a_rate[:, None] * step_size, upto, precision=HIGHEST)
    to_end = jnp.exp(cumulative[:, -1:] - cumulative) * step_size

    def over_heads(per_head):
        return jnp.broadcast_to(per_head.T[:, :, None], (tok_rows, heads, HP)).reshape(tok_rows, head_rows)

    local = lax.dot_general(
        inputs * over_heads(to_end), b_cols, (((0,), (1,)), ((), ())), precision=HIGHEST
    )
    log_block = cumulative[:, -1]
    log_high = log_block.astype(BF16)
    log_low = (log_block - log_high.astype(F32)).astype(BF16)
    log_rows = jnp.broadcast_to(jnp.concatenate([log_high, log_low])[:, None], (2 * heads, NSTATE))
    pair = jnp.concatenate([key, value], axis=0)
    pair_other = lax.ppermute(pair, "seq", [(0, 1), (1, 0)])
    message = jnp.concatenate([pair, pair_other, local.astype(BF16), log_rows], axis=0)
    gathered = lax.all_gather(message, "row", axis=0, tiled=False)

    pairs = jnp.stack([gathered[:, : 2 * HD], gathered[:, 2 * HD : 4 * HD]])
    keys = pairs[:, :, :HD].transpose(2, 0, 1, 3).reshape(HD, -1)
    values = pairs[:, :, HD:].reshape(-1, HD)
    places = jnp.arange(ROWS, dtype=jnp.int32)
    key_start = jnp.concatenate([seq * half_rows + places * tok_rows, (1 - seq) * half_rows + places * tok_rows])
    query_start = seq * half_rows + row * tok_rows
    attn_out = attention(query, query_start, keys, values, key_start)

    states = gathered[:, 4 * HD : 4 * HD + head_rows].astype(F32).reshape(ROWS, heads, HP, NSTATE)
    logs = gathered[:, 4 * HD + head_rows :, 0].astype(F32)
    logs = logs[:, :heads] + logs[:, heads:]
    later = places[None, :] > places[:, None]
    ahead = places < row
    log_to_end = jnp.sum(jnp.where(later[:, :, None], logs[None], 0.0), axis=1)
    log_between = jnp.sum(jnp.where((later & ahead[None, :])[:, :, None], logs[None], 0.0), axis=1)
    log_ahead = jnp.sum(jnp.where(ahead[:, None], logs, 0.0), axis=0)
    half_end = jnp.sum(jnp.exp(log_to_end)[:, :, None, None] * states, axis=0)
    earlier_half = lax.ppermute(half_end.astype(BF16), "seq", [(0, 1)]).astype(F32)
    weight = jnp.where(ahead[:, None], jnp.exp(log_between), 0.0)
    prior = jnp.sum(weight[:, :, None, None] * states, axis=0)
    prior = prior + jnp.exp(log_ahead)[:, None, None] * earlier_half

    lower = position[:, None] >= position[None, :]
    inner = lax.dot_general(c_cols, b_cols, (((0,), (0,)), ((), ())), precision=HIGHEST)
    decays = jnp.exp(jnp.where(lower[None], cumulative[:, :, None] - cumulative[:, None, :], -jnp.inf))
    coefficient = inner[None] * decays * step_size[:, None, :]
    within = jnp.einsum("htu,uhp->thp", coefficient, inputs.reshape(tok_rows, heads, HP), precision=HIGHEST)
    carried = lax.dot_general(
        c_cols, prior.reshape(head_rows, NSTATE), (((0,), (1,)), ((), ())), precision=HIGHEST
    )
    result = within.reshape(tok_rows, -1) + over_heads(jnp.exp(cumulative)) * carried
    result = result + jnp.repeat(d_skip, HP)[None, :] * inputs
    gated = (result * jax.nn.silu(gate_raw)).reshape(tok_rows, heads, HP)
    normed = gated * lax.rsqrt(jnp.mean(gated * gated, axis=-1, keepdims=True) + 1e-05)
    ssm_out = normed.reshape(tok_rows, head_rows).astype(BF16)

    mixer = lax.all_gather(jnp.concatenate([attn_out, ssm_out], axis=1), "row", axis=0, tiled=True)
    w_out = jnp.concatenate([w_attn_out, w_ssm_out], axis=0)
    terms = jnp.dot(mixer, w_out, preferred_element_type=F32)
    parts = terms.astype(BF16).reshape(COLS, -1, terms.shape[1])
    swapped = lax.all_to_all(parts, "col", 0, 0, tiled=True)
    return jnp.sum(swapped.astype(F32), axis=0).astype(BF16)


def solution(mesh):
    in_specs = (
        P("seq", "row"),
        P("row", "col"),
        P("row", "col"),
        P("row", "col"),
        P("row", "col"),
        P("row", "col"),
        P("row", None),
        P("row", "col"),
        P("col"),
        P("col"),
        P("col"),
        P("col", "row"),
        P("col", "row"),
    )
    out_specs = P(("seq", "col"), "row")
    return jax.shard_map(
        on_device, mesh=mesh, in_specs=in_specs, out_specs=out_specs, check_vma=False
    )
```

time: 637 us -> 240 us (0.38)
  waiting for transfers between devices: 467 us -> 114 us
  blocking collectives: 99.6 us -> 24.7 us
  starting transfers between devices: 0.4 us -> 29.4 us
  matrix products: 37.8 us -> 30.5 us
  other arithmetic: 5.12 us -> 12.2 us
    all_gather x10 -> x2, waiting for transfers between devices: 388 us -> 79.8 us  [the longest x1 41 us: on_device(): lax.all_gather(jnp.concatenate([attn_out, ssm_out], axis=1), 'row', axis=...]
    reduce_scatter x1 -> x0, waiting for transfers between devices: 75.7 us -> none  [on_device(): lax.psum_scatter(terms.astype(jnp.bfloat16), 'col', scatter_dimension=0,...]
    all_gather x2 -> x0, blocking collectives: 49.5 us -> none  [the longest x1 33.6 us: carried_in(): lax.all_gather(a.astype(kind), axis)]
    ppermute x0 -> x19, waiting for transfers between devices: none -> 34.4 us  [the longest x14 32.7 us: ring_step(): lax.ppermute(array, 'row', [(i, (i + 2 * step) % ROWS) for i in range(ROW...]
    ppermute x0 -> x19, starting transfers between devices: none -> 29.2 us  [the longest x14 20.9 us: ring_step(): lax.ppermute(array, 'row', [(i, (i + 2 * step) % ROWS) for i in range(ROW...]
    all_to_all x1, blocking collectives: 50.1 us -> 24.7 us  [on_device(): swapped = lax.all_to_all(parts, 'col', 0, 0, tiled=True)]
    dot_general x1 -> x0, local copies, waits for them, and re-layouts: 7.96 us -> none  [on_device(): jnp.dot(own_tokens, piece, preferred_element_type=jnp.float32)]
    dot_general x15 -> x24, matrix products: 37.8 us -> 30.5 us  [the longest x8 14.3 us: project_narrow(): return jnp.dot(blocks[hop], w_narrow, preferred_element_type=F32)]
  transfers between devices with their start and end apart: 11 -> 21, of which waited for: 10 -> 9; matrix products, arithmetic and copies ran while one was open for 8% -> 15% of each run, Pallas kernels for 0% -> 0%
where the time goes in v1:
time: 240 us
  waiting for transfers between devices  114 us (48%)
  matrix products  30.5 us (13%)
  starting transfers between devices  29.4 us (12%)
  blocking collectives  24.7 us (10%)
  local copies, waits for them, and re-layouts  14.3 us (6%)
  between operations  14.2 us (6%)
  other arithmetic  12.2 us (5%)
    all_gather x1, waiting for transfers between devices, on_device(): lax.all_gather(jnp.concatenate([attn_out, ssm_out], axis=1), 'row', axis=...  41 us
    all_gather x1, waiting for transfers between devices, on_device(): gathered = lax.all_gather(message, 'row', axis=0, tiled=False)  38.8 us
    ppermute x14, waiting for transfers between devices, ring_step(): lax.ppermute(array, 'row', [(i, (i + 2 * step) % ROWS) for i in range(ROW...  32.7 us
    all_to_all x1, blocking collectives, on_device(): swapped = lax.all_to_all(parts, 'col', 0, 0, tiled=True)  24.7 us
    ppermute x14, starting transfers between devices, ring_step(): lax.ppermute(array, 'row', [(i, (i + 2 * step) % ROWS) for i in range(ROW...  20.9 us
    dot_general x8, matrix products, project_narrow(): return jnp.dot(blocks[hop], w_narrow, preferred_element_type=F32)  14.3 us
    unnamed x36, local copies, waits for them, and re-layouts  5.12 us
  transfers between devices with their start and end apart: 21, of which 9 were waited for; matrix products, arithmetic and copies ran while one was open for 15% of the time, Pallas kernels for 0%

profile of v1, /device:TPU:1, one launch (start us, length us, event | category | flops | bytes accessed | tf_op | source)
XLA Modules:
  0.0 239.5 jit_solution(3481005113200811382)
XLA Ops:
  6.5 3.2 %collective-permute-start.1 = (bf16[2048,320]{0,1:T(8,128)(2,1)}, bf16[2048,320]{0,1:T(8,128)(2,1)}, u32[]{:S(2)}, u32[]{:S(2)}) collective-permute-start(bf16[2048,320]{0,1:T(8,128)(2,1)} %param.13), channel_id=1, source_target_pairs={{0,8},{8,0},{16,24},{24,16},{32,40},{40,32},{48,56},{56,48},{64,72... | collective-permute-start | bytes 3932168 | tf_op jit(solution)/shard_map/ppermute | solution.py:22
  13.6 1.8 constant_dynamic-update-slice_fusion.1
  18.8 1.8 convolution_convert_fusion.1
  20.6 3.9 %collective-permute-start.13 = (bf16[128,1152]{1,0:T(8,128)(2,1)S(1)}, bf16[128,1152]{1,0:T(8,128)(2,1)S(1)}, u32[]{:S(2)}, u32[]{:S(2)}) collective-permute-start(bf16[128,1152]{1,0:T(8,128)(2,1)S(1)} %convolution_convert_fusion.1), channel_id=1, source_target_pairs={{0,112},{8,120},{16,0},{24,8},{32,16},{40,24},{48,32},{56,40},{64,... | collective-permute-start | bytes 884744 | tf_op jit(solution)/shard_map/ppermute | solution.py:18
  25.1 1.8 convolution_convert_fusion.2
  27.5 2.7 %collective-permute-start.6 = (f32[904,128]{1,0:T(8,128)S(1)}, f32[904,128]{1,0:T(8,128)S(1)}, u32[]{:S(2)}, u32[]{:S(2)}) collective-permute-start(f32[904,128]{1,0:T(8,128)S(1)} %fusion.34), channel_id=1, source_target_pairs={{0,112},{8,120},{16,0},{24,8},{32,16},{40,24},{48,32},{56,40},{64,... | collective-permute-start | bytes 1388552 | tf_op jit(solution)/shard_map/ppermute | solution.py:18
  30.8 1.8 add_convert_fusion.2
  32.6 3.2 %collective-permute-start.14 = (bf16[128,1152]{1,0:T(8,128)(2,1)S(1)}, bf16[128,1152]{1,0:T(8,128)(2,1)S(1)}, u32[]{:S(2)}, u32[]{:S(2)}) collective-permute-start(bf16[128,1152]{1,0:T(8,128)(2,1)S(1)} %add_convert_fusion.2), channel_id=1, source_target_pairs={{0,112},{8,120},{16,0},{24,8},{32,16},{40,24},{48,32},{56,40},{64,... | collective-permute-start | bytes 884744 | tf_op jit(solution)/shard_map/ppermute | solution.py:18
  36.4 1.8 add_convert_fusion.4
  38.3 7.7 %collective-permute-done.2 = f32[904,128]{1,0:T(8,128)S(1)} collective-permute-done((f32[904,128]{1,0:T(8,128)S(1)}, f32[904,128]{1,0:T(8,128)S(1)}, u32[]{:S(2)}, u32[]{:S(2)}) %collective-permute-start.2) | collective-permute-done | bytes 462880 | tf_op jit(solution)/shard_map/ppermute | solution.py:18
  46.8 1.8 add_convert_fusion.1
  48.5 3.5 %collective-permute-start.15 = (bf16[128,1152]{1,0:T(8,128)(2,1)S(1)}, bf16[128,1152]{1,0:T(8,128)(2,1)S(1)}, u32[]{:S(2)}, u32[]{:S(2)}) collective-permute-start(bf16[128,1152]{1,0:T(8,128)(2,1)S(1)} %add_convert_fusion.1), channel_id=1, source_target_pairs={{0,112},{8,120},{16,0},{24,8},{32,16},{40,24},{48,32},{56,40},{64,... | collective-permute-start | bytes 884744 | tf_op jit(solution)/shard_map/ppermute | solution.py:18
  52.8 1.8 add_convert_fusion.3
  56.1 6.2 %collective-permute-done.3 = f32[904,128]{1,0:T(8,128)S(1)} collective-permute-done((f32[904,128]{1,0:T(8,128)S(1)}, f32[904,128]{1,0:T(8,128)S(1)}, u32[]{:S(2)}, u32[]{:S(2)}) %collective-permute-start.3) | collective-permute-done | bytes 462880 | tf_op jit(solution)/shard_map/ppermute | solution.py:18
  62.4 1.8 add_convert_fusion
  64.2 2.7 %collective-permute-start.16 = (bf16[128,1152]{1,0:T(8,128)(2,1)S(1)}, bf16[128,1152]{1,0:T(8,128)(2,1)S(1)}, u32[]{:S(2)}, u32[]{:S(2)}) collective-permute-start(bf16[128,1152]{1,0:T(8,128)(2,1)S(1)} %add_convert_fusion), channel_id=1, source_target_pairs={{0,112},{8,120},{16,0},{24,8},{32,16},{40,24},{48,32},{56,40},{64,... | collective-permute-start | bytes 884744 | tf_op jit(solution)/shard_map/ppermute | solution.py:18
  67.6 2.5 %collective-permute-start.8 = (f32[904,128]{1,0:T(8,128)S(1)}, f32[904,128]{1,0:T(8,128)S(1)}, u32[]{:S(2)}, u32[]{:S(2)}) collective-permute-start(f32[904,128]{1,0:T(8,128)S(1)} %add.312), channel_id=1, source_target_pairs={{0,112},{8,120},{16,0},{24,8},{32,16},{40,24},{48,32},{56,40},{64,... | collective-permute-start | bytes 1388552 | tf_op jit(solution)/shard_map/ppermute | solution.py:18
  70.1 8.4 %collective-permute-done.4 = f32[904,128]{1,0:T(8,128)S(1)} collective-permute-done((f32[904,128]{1,0:T(8,128)S(1)}, f32[904,128]{1,0:T(8,128)S(1)}, u32[]{:S(2)}, u32[]{:S(2)}) %collective-permute-start.4) | collective-permute-done | bytes 462880 | tf_op jit(solution)/shard_map/ppermute | solution.py:18
  78.7 1.8 fusion.3
  80.5 2.5 %collective-permute-done.8 = f32[904,128]{1,0:T(8,128)S(1)} collective-permute-done((f32[904,128]{1,0:T(8,128)S(1)}, f32[904,128]{1,0:T(8,128)S(1)}, u32[]{:S(2)}, u32[]{:S(2)}) %collective-permute-start.8) | collective-permute-done | bytes 462880 | tf_op jit(solution)/shard_map/ppermute | solution.py:18
  83.0 7.5 %collective-permute-done.5 = f32[904,128]{1,0:T(8,128)S(1)} collective-permute-done((f32[904,128]{1,0:T(8,128)S(1)}, f32[904,128]{1,0:T(8,128)S(1)}, u32[]{:S(2)}, u32[]{:S(2)}) %collective-permute-start.5) | collective-permute-done | bytes 462880 | tf_op jit(solution)/shard_map/ppermute | solution.py:18
  93.4 1.8 collective-permute-done.17
  101.1 38.8 %all-gather.6.cloned.1.call-done = bf16[16640,128]{1,0:T(8,128)(2,1)} async-done(((bf16[1040,128]{1,0:T(8,128)(2,1)}), bf16[16640,128]{1,0:T(8,128)(2,1)}) %all-gather.6.cloned.1.call-update) | async-done | bytes 4259856 | tf_op jit(solution)/shard_map/all_gather | solution.py:135
  140.7 1.7 slice_bitcast_fusion.1
  145.7 4.0 %fusion.2 = (bf16[512,128]{1,0:T(8,128)(2,1)S(1)}, f32[512,128]{1,0:T(8,128)S(1)}) fusion(f32[16,512]{1,0:T(8,128)S(1)} %mul.216, bf16[16,1040,128]{2,1,0:T(8,128)(2,1)} %bitcast.64, f32[16,512]{1,0:T(8,128)S(1)} %mul.211), kind=kLoop, calls=%fused_computation.7 | loop fusion | flops 5111808 | bytes 2555904 | tf_op jit(solution)/shard_map/reduce_sum | solution.py:153
  149.7 3.1 %collective-permute-start.18 = (bf16[8,64,128]{2,1,0:T(8,128)(2,1)S(1)}, bf16[8,64,128]{2,1,0:T(8,128)(2,1)S(1)}, u32[]{:S(2)}, u32[]{:S(2)}) collective-permute-start(bf16[8,64,128]{2,1,0:T(8,128)(2,1)S(1)} %bitcast.75), channel_id=1, source_target_pairs={{0,128},{1,129},{2,130},{3,131},{4,132},{5,133},{6,134},{7,135},{8... | collective-permute-start | bytes 393224 | tf_op jit(solution)/shard_map/ppermute | solution.py:154
  152.9 1.8 fusion
  154.7 2.3 convert_reduce_fusion
  157.0 2.3 fusion.10
  162.3 41.0 %all-gather.4.cloned.1.call-done = bf16[2048,1024]{1,0:T(8,128)(2,1)} async-done(((bf16[128,1024]{1,0:T(8,128)(2,1)}), bf16[2048,1024]{1,0:T(8,128)(2,1)}) %all-gather.4.cloned.1.call-update) | async-done | bytes 4194320 | tf_op jit(solution)/shard_map/all_gather | solution.py:173
  203.3 3.7 %convolution_convert_fusion = bf16[2048,320]{0,1:T(8,128)(2,1)S(1)} fusion(bf16[2048,1024]{1,0:T(8,128)(2,1)} %all-gather.4.cloned.1.call-done, bf16[512,320]{0,1:T(8,128)(2,1)S(1)} %copy-done.12, bf16[512,320]{0,1:T(8,128)(2,1)S(1)} %copy-done.13), kind=kOutput, calls=%fused_computation.8 | convolution fusion | flops 1344143360 | bytes 6160384 | tf_op jit(solution)/shard_map/dot_general | solution.py:175
  207.1 24.7 %all_to_all.5 = bf16[8,256,320]{1,2,0:T(8,128)(2,1)S(1)} all-to-all(bf16[8,256,320]{1,2,0:T(8,128)(2,1)S(1)} %bitcast.61), channel_id=1, replica_groups=mesh['seq'=2,'row'=16,'col'=8] {'col'}, dimensions={0} | all-to-all | bytes 2621440 | tf_op jit(solution)/shard_map/all_to_all | solution.py:177
  (140 shorter events, 30.0 us)
Async XLA Ops:
  6.5 10.0 %copy-start.5 = (bf16[2048,320]{0,1:T(8,128)(2,1)S(1)}, bf16[2048,320]{0,1:T(8,128)(2,1)}, u32[]{:S(2)}) copy-start(bf16[2048,320]{0,1:T(8,128)(2,1)} %param.13) | copy-start | bytes 3932164
  6.5 133.3 %all-gather.6.cloned.1.call-start = ((), (), s32[]{:S(2)}) async-start(), calls=%async_computation.2 | async-start | bytes 4526080 | tf_op jit(solution)/shard_map/all_gather | solution.py:135
  6.5 10.4 %collective-permute-start.1 = (bf16[2048,320]{0,1:T(8,128)(2,1)}, bf16[2048,320]{0,1:T(8,128)(2,1)}, u32[]{:S(2)}, u32[]{:S(2)}) collective-permute-start(bf16[2048,320]{0,1:T(8,128)(2,1)} %param.13), channel_id=1, source_target_pairs={{0,8},{8,0},{16,24},{24,16},{32,40},{40,32},{48,56},{56,48},{64,72... | collective-permute-start | bytes 3932168 | tf_op jit(solution)/shard_map/ppermute | solution.py:22
  10.6 4.8 %copy-start.6 = (bf16[320,512]{1,0:T(8,128)(2,1)S(1)}, bf16[320,512]{1,0:T(8,128)(2,1)}, u32[]{:S(2)}) copy-start(bf16[320,512]{1,0:T(8,128)(2,1)} %param.18) | copy-start | bytes 983044
  10.6 6.1 %copy-start = (bf16[320,512]{1,0:T(8,128)(2,1)S(1)}, bf16[320,512]{1,0:T(8,128)(2,1)}, u32[]{:S(2)}) copy-start(bf16[320,512]{1,0:T(8,128)(2,1)} %param.14) | copy-start | bytes 983044
  10.6 6.1 %copy-start.2 = (bf16[320,256]{1,0:T(8,128)(2,1)S(1)}, bf16[320,256]{1,0:T(8,128)(2,1)}, u32[]{:S(2)}) copy-start(bf16[320,256]{1,0:T(8,128)(2,1)} %param.19) | copy-start | bytes 491524
  10.6 6.1 %copy-start.4 = (bf16[320,128]{1,0:T(8,128)(2,1)S(1)}, bf16[320,128]{1,0:T(8,128)(2,1)}, u32[]{:S(2)}) copy-start(bf16[320,128]{1,0:T(8,128)(2,1)} %param.15) | copy-start | bytes 245764
  11.9 4.8 %collective-permute-start = (bf16[320,904]{1,0:T(8,128)(2,1)S(1)}, bf16[320,904]{1,0:T(8,128)(2,1)S(1)}, u32[]{:S(2)}, u32[]{:S(2)}) collective-permute-start(bf16[320,904]{1,0:T(8,128)(2,1)S(1)} %pad_maximum_fusion.3), channel_id=1, source_target_pairs={{0,8},{8,0},{16,24},{24,16},{32,40},{40,32},{48,56},{56,48},{64,72... | collective-permute-start | bytes 1735688 | tf_op jit(solution)/shard_map/ppermute | solution.py:22
  16.2 2.6 %collective-permute-start.9 = (bf16[320,1152]{1,0:T(8,128)(2,1)}, bf16[320,1152]{1,0:T(8,128)(2,1)}, u32[]{:S(2)}, u32[]{:S(2)}) collective-permute-start(bf16[320,1152]{1,0:T(8,128)(2,1)} %constant_dynamic-update-slice_fusion), channel_id=1, source_target_pairs={{0,8},{8,0},{16,24},{24,16},{32,40},{40,32},{48,56},{56,48},{64,72... | collective-permute-start | bytes 2211848 | tf_op jit(solution)/shard_map/ppermute | solution.py:22
  20.6 10.2 %collective-permute-start.13 = (bf16[128,1152]{1,0:T(8,128)(2,1)S(1)}, bf16[128,1152]{1,0:T(8,128)(2,1)S(1)}, u32[]{:S(2)}, u32[]{:S(2)}) collective-permute-start(bf16[128,1152]{1,0:T(8,128)(2,1)S(1)} %convolution_convert_fusion.1), channel_id=1, source_target_pairs={{0,112},{8,120},{16,0},{24,8},{32,16},{40,24},{48,32},{56,40},{64,... | collective-permute-start | bytes 884744 | tf_op jit(solution)/shard_map/ppermute | solution.py:18
  26.9 9.6 %collective-permute-start.10 = (bf16[128,1152]{1,0:T(8,128)(2,1)S(1)}, bf16[128,1152]{1,0:T(8,128)(2,1)S(1)}, u32[]{:S(2)}, u32[]{:S(2)}) collective-permute-start(bf16[128,1152]{1,0:T(8,128)(2,1)S(1)} %convolution_convert_fusion.2), channel_id=1, source_target_pairs={{0,16},{8,24},{16,32},{24,40},{32,48},{40,56},{48,64},{56,72},{64,... | collective-permute-start | bytes 884744 | tf_op jit(solution)/shard_map/ppermute | solution.py:18
  27.5 25.1 %collective-permute-start.6 = (f32[904,128]{1,0:T(8,128)S(1)}, f32[904,128]{1,0:T(8,128)S(1)}, u32[]{:S(2)}, u32[]{:S(2)}) collective-permute-start(f32[904,128]{1,0:T(8,128)S(1)} %fusion.34), channel_id=1, source_target_pairs={{0,112},{8,120},{16,0},{24,8},{32,16},{40,24},{48,32},{56,40},{64,... | collective-permute-start | bytes 1388552 | tf_op jit(solution)/shard_map/ppermute | solution.py:18
  30.2 15.8 %collective-permute-start.2 = (f32[904,128]{1,0:T(8,128)S(1)}, f32[904,128]{1,0:T(8,128)S(1)}, u32[]{:S(2)}, u32[]{:S(2)}) collective-permute-start(f32[904,128]{1,0:T(8,128)S(1)} %fusion.40), channel_id=1, source_target_pairs={{0,16},{8,24},{16,32},{24,40},{32,48},{40,56},{48,64},{56,72},{64,... | collective-permute-start | bytes 1388552 | tf_op jit(solution)/shard_map/ppermute | solution.py:18
  32.6 14.1 %collective-permute-start.14 = (bf16[128,1152]{1,0:T(8,128)(2,1)S(1)}, bf16[128,1152]{1,0:T(8,128)(2,1)S(1)}, u32[]{:S(2)}, u32[]{:S(2)}) collective-permute-start(bf16[128,1152]{1,0:T(8,128)(2,1)S(1)} %add_convert_fusion.2), channel_id=1, source_target_pairs={{0,112},{8,120},{16,0},{24,8},{32,16},{40,24},{48,32},{56,40},{64,... | collective-permute-start | bytes 884744 | tf_op jit(solution)/shard_map/ppermute | solution.py:18
  38.2 14.5 %collective-permute-start.11 = (bf16[128,1152]{1,0:T(8,128)(2,1)S(1)}, bf16[128,1152]{1,0:T(8,128)(2,1)S(1)}, u32[]{:S(2)}, u32[]{:S(2)}) collective-permute-start(bf16[128,1152]{1,0:T(8,128)(2,1)S(1)} %add_convert_fusion.4), channel_id=1, source_target_pairs={{0,16},{8,24},{16,32},{24,40},{32,48},{40,56},{48,64},{56,72},{64,... | collective-permute-start | bytes 884744 | tf_op jit(solution)/shard_map/ppermute | solution.py:18
  46.1 16.2 %collective-permute-start.3 = (f32[904,128]{1,0:T(8,128)S(1)}, f32[904,128]{1,0:T(8,128)S(1)}, u32[]{:S(2)}, u32[]{:S(2)}) collective-permute-start(f32[904,128]{1,0:T(8,128)S(1)} %add.287), channel_id=1, source_target_pairs={{0,16},{8,24},{16,32},{24,40},{32,48},{40,56},{48,64},{56,72},{64,... | collective-permute-start | bytes 1388552 | tf_op jit(solution)/shard_map/ppermute | solution.py:18
  48.5 13.9 %collective-permute-start.15 = (bf16[128,1152]{1,0:T(8,128)(2,1)S(1)}, bf16[128,1152]{1,0:T(8,128)(2,1)S(1)}, u32[]{:S(2)}, u32[]{:S(2)}) collective-permute-start(bf16[128,1152]{1,0:T(8,128)(2,1)S(1)} %add_convert_fusion.1), channel_id=1, source_target_pairs={{0,112},{8,120},{16,0},{24,8},{32,16},{40,24},{48,32},{56,40},{64,... | collective-permute-start | bytes 884744 | tf_op jit(solution)/shard_map/ppermute | solution.py:18
  52.7 14.9 %collective-permute-start.7 = (f32[904,128]{1,0:T(8,128)S(1)}, f32[904,128]{1,0:T(8,128)S(1)}, u32[]{:S(2)}, u32[]{:S(2)}) collective-permute-start(f32[904,128]{1,0:T(8,128)S(1)} %add.307), channel_id=1, source_target_pairs={{0,112},{8,120},{16,0},{24,8},{32,16},{40,24},{48,32},{56,40},{64,... | collective-permute-start | bytes 1388552 | tf_op jit(solution)/shard_map/ppermute | solution.py:18
  54.6 24.1 %collective-permute-start.12 = (bf16[128,1152]{1,0:T(8,128)(2,1)S(1)}, bf16[128,1152]{1,0:T(8,128)(2,1)S(1)}, u32[]{:S(2)}, u32[]{:S(2)}) collective-permute-start(bf16[128,1152]{1,0:T(8,128)(2,1)S(1)} %add_convert_fusion.3), channel_id=1, source_target_pairs={{0,16},{8,24},{16,32},{24,40},{32,48},{40,56},{48,64},{56,72},{64,... | collective-permute-start | bytes 884744 | tf_op jit(solution)/shard_map/ppermute | solution.py:18
  62.3 16.2 %collective-permute-start.4 = (f32[904,128]{1,0:T(8,128)S(1)}, f32[904,128]{1,0:T(8,128)S(1)}, u32[]{:S(2)}, u32[]{:S(2)}) collective-permute-start(f32[904,128]{1,0:T(8,128)S(1)} %add.292), channel_id=1, source_target_pairs={{0,16},{8,24},{16,32},{24,40},{32,48},{40,56},{48,64},{56,72},{64,... | collective-permute-start | bytes 1388552 | tf_op jit(solution)/shard_map/ppermute | solution.py:18
  64.2 14.4 %copy-start.14 = (f32[8]{0:T(128)S(1)}, f32[8]{0:T(128)}, u32[]{:S(2)}) copy-start(f32[8]{0:T(128)} %param.22) | copy-start | bytes 100
  64.2 14.5 %collective-permute-start.16 = (bf16[128,1152]{1,0:T(8,128)(2,1)S(1)}, bf16[128,1152]{1,0:T(8,128)(2,1)S(1)}, u32[]{:S(2)}, u32[]{:S(2)}) collective-permute-start(bf16[128,1152]{1,0:T(8,128)(2,1)S(1)} %add_convert_fusion), channel_id=1, source_target_pairs={{0,112},{8,120},{16,0},{24,8},{32,16},{40,24},{48,32},{56,40},{64,... | collective-permute-start | bytes 884744 | tf_op jit(solution)/shard_map/ppermute | solution.py:18
  67.6 15.4 %collective-permute-start.8 = (f32[904,128]{1,0:T(8,128)S(1)}, f32[904,128]{1,0:T(8,128)S(1)}, u32[]{:S(2)}, u32[]{:S(2)}) collective-permute-start(f32[904,128]{1,0:T(8,128)S(1)} %add.312), channel_id=1, source_target_pairs={{0,112},{8,120},{16,0},{24,8},{32,16},{40,24},{48,32},{56,40},{64,... | collective-permute-start | bytes 1388552 | tf_op jit(solution)/shard_map/ppermute | solution.py:18
  78.6 11.9 %collective-permute-start.5 = (f32[904,128]{1,0:T(8,128)S(1)}, f32[904,128]{1,0:T(8,128)S(1)}, u32[]{:S(2)}, u32[]{:S(2)}) collective-permute-start(f32[904,128]{1,0:T(8,128)S(1)} %add.297), channel_id=1, source_target_pairs={{0,16},{8,24},{16,32},{24,40},{32,48},{40,56},{48,64},{56,72},{64,... | collective-permute-start | bytes 1388552 | tf_op jit(solution)/shard_map/ppermute | solution.py:18
  80.5 17.2 %copy-start.9 = (f32[128,1152]{1,0:T(8,128)}, f32[128,1152]{1,0:T(8,128)S(1)}, u32[]{:S(2)}) copy-start(f32[128,1152]{1,0:T(8,128)S(1)} %fusion.3) | copy-start | bytes 1769476
  80.5 10.6 %copy-start.10 = (f32[8]{0:T(128)S(1)}, f32[8]{0:T(128)}, u32[]{:S(2)}) copy-start(f32[8]{0:T(128)} %param.21) | copy-start | bytes 100
  91.1 5.9 %copy-start.11 = (f32[8]{0:T(128)S(1)}, f32[8]{0:T(128)}, u32[]{:S(2)}) copy-start(f32[8]{0:T(128)} %param.23) | copy-start | bytes 100
  91.9 3.2 %collective-permute-start.17 = (bf16[256,128]{1,0:T(8,128)(2,1)S(1)}, bf16[256,128]{1,0:T(8,128)(2,1)S(1)}, u32[]{:S(2)}, u32[]{:S(2)}) collective-permute-start(bf16[256,128]{1,0:T(8,128)(2,1)S(1)} %pad_maximum_fusion.39), channel_id=1, source_target_pairs={{0,128},{128,0},{1,129},{129,1},{2,130},{130,2},{3,131},{131,3},{4... | collective-permute-start | bytes 196616 | tf_op jit(solution)/shard_map/ppermute | solution.py:133
  96.7 106.6 %all-gather.4.cloned.1.call-start = ((), (), s32[]{:S(2)}) async-start(), calls=%async_computation.1 | async-start | bytes 4456448 | tf_op jit(solution)/shard_map/all_gather | solution.py:173
  149.7 9.7 %collective-permute-start.18 = (bf16[8,64,128]{2,1,0:T(8,128)(2,1)S(1)}, bf16[8,64,128]{2,1,0:T(8,128)(2,1)S(1)}, u32[]{:S(2)}, u32[]{:S(2)}) collective-permute-start(bf16[8,64,128]{2,1,0:T(8,128)(2,1)S(1)} %bitcast.75), channel_id=1, source_target_pairs={{0,128},{1,129},{2,130},{3,131},{4,132},{5,133},{6,134},{7,135},{8... | collective-permute-start | bytes 393224 | tf_op jit(solution)/shard_map/ppermute | solution.py:154
  161.1 42.2 %copy-start.12 = (bf16[512,320]{0,1:T(8,128)(2,1)S(1)}, bf16[512,320]{0,1:T(8,128)(2,1)}, u32[]{:S(2)}) copy-start(bf16[512,320]{0,1:T(8,128)(2,1)} %param.25) | copy-start | bytes 983044
  161.1 42.2 %copy-start.13 = (bf16[512,320]{0,1:T(8,128)(2,1)S(1)}, bf16[512,320]{0,1:T(8,128)(2,1)}, u32[]{:S(2)}) copy-start(bf16[512,320]{0,1:T(8,128)(2,1)} %param.24) | copy-start | bytes 983044
  (4 other events, 8.1 us)
Sparse Core Ops, SparseCore 0:
  96.8 43.0 all-gather.5
  162.4 40.8 all-gather.3

commit v2 on v1

v2 whole, which is shorter than its diff:
```python
import jax
import jax.numpy as jnp
from jax import lax
from jax.experimental import pallas as pl
from jax.experimental.pallas import tpu as pltpu
from jax.sharding import PartitionSpec as P

HD = 128
HP = 64
NSTATE = 128
RING = 8
ROWS = 16
COLS = 8
TOK = 128
F32 = jnp.float32
BF16 = jnp.bfloat16
HIGHEST = lax.Precision.HIGHEST
VMEM_LIMIT = 48 * 1024 * 1024


def ring_step(array, step):
    return lax.ppermute(array, "row", [(i, (i + 2 * step) % ROWS) for i in range(ROWS)])


def other_core(array):
    return lax.ppermute(array, "row", [(i, i ^ 1) for i in range(ROWS)])


def after(value, *others):
    return lax.optimization_barrier((value,) + others)[0]


class Reduce:
    def __init__(self, term, wire, right_hops):
        self.term = term
        self.wire = wire
        self.limits = (right_hops, RING - 1 - right_hops)
        self.held = [None, None]
        self.sent = ()

    def hop(self, hop, *earlier):
        now = {}
        for way, sign in ((0, 1), (1, -1)):
            if hop <= self.limits[way]:
                term = self.term(sign * hop, *earlier)
                if self.held[way] is not None:
                    term = self.held[way].astype(F32) + term
                now[way] = term.astype(self.wire)
        for way, sign in ((1, -1), (0, 1)):
            if way in now:
                self.held[way] = ring_step(now[way], sign)
        self.sent = tuple(now.values())

    def result(self):
        return self.term(0) + self.held[0].astype(F32) + self.held[1].astype(F32)


def by_rows(weight, tokens):
    return lax.dot_general(weight, tokens, (((0,), (1,)), ((), ())), preferred_element_type=F32)


def nt_dot(a, b):
    return lax.dot_general(a, b, (((1,), (1,)), ((), ())), preferred_element_type=F32)


def tn_dot(a, b):
    return lax.dot_general(a, b, (((0,), (0,)), ((), ())), preferred_element_type=F32)


def scan_kernel(place_ref, ug_ref, own_ref, rate_ref, skip_ref, y_ref, state_ref, cum_ref):
    chunks, heads = own_ref.shape[0], RING
    chip = place_ref[0]
    first = own_ref.shape[2] - 2 * heads
    steps = []
    for j in range(chunks):
        rows = own_ref[j, 0, first:].astype(F32)
        mine = lax.broadcasted_iota(jnp.int32, rows.shape, 0) % heads == chip
        steps.append(jnp.sum(jnp.where(mine, rows, 0.0), axis=0, keepdims=True))
    step_all = jnp.concatenate(steps, axis=0)
    ahead = lax.broadcasted_iota(jnp.int32, (TOK, TOK), 0)
    behind = lax.broadcasted_iota(jnp.int32, (TOK, TOK), 1)
    upto = (ahead <= behind).astype(F32)
    cum_all = jnp.dot(-rate_ref[chip] * step_all, upto, precision=HIGHEST, preferred_element_type=F32)
    cum_ref[...] = cum_all
    columns = jnp.concatenate([cum_all, step_all], axis=0).T
    skip = skip_ref[chip]
    state = jnp.zeros((HP, NSTATE), F32)
    for j in range(chunks):
        raw = ug_ref[j * TOK : (j + 1) * TOK, :].T[:HP]
        inputs = raw / (1.0 + jnp.exp(-raw))
        b_cols = own_ref[j, 0, 4 * HD : 4 * HD + NSTATE]
        c_cols = own_ref[j, 0, 4 * HD + NSTATE : 4 * HD + 2 * NSTATE]
        step = step_all[j : j + 1, :]
        cum = cum_all[j : j + 1, :]
        end = cum_all[j : j + 1, TOK - 1 : TOK]
        cum_column = columns[:, j : j + 1]
        step_column = columns[:, chunks + j : chunks + j + 1]
        decay = jnp.exp(jnp.where(ahead <= behind, cum - cum_column, -1e30))
        mix = tn_dot(b_cols, c_cols) * decay * step_column
        y = jnp.dot(inputs.astype(BF16), mix.astype(BF16), preferred_element_type=F32)
        if j:
            y = y + jnp.exp(cum) * jnp.dot(state.astype(BF16), c_cols, preferred_element_type=F32)
        y_ref[j] = y + skip * inputs
        weighted = inputs * (jnp.exp(end - cum) * step)
        state = jnp.exp(end) * state + nt_dot(weighted.astype(BF16), b_cols)
    state_ref[:HP] = state
    total = jnp.sum(cum_all[:, TOK - 1 : TOK], axis=0, keepdims=True)
    state_ref[HP:] = jnp.broadcast_to(total, (8, NSTATE))


def finish_kernel(place_ref, ug_ref, own_ref, cum_ref, y_ref, state_ref, out_ref):
    state = state_ref[...].astype(BF16)
    before = jnp.zeros((1, 1), F32)
    for j in range(own_ref.shape[0]):
        gate = ug_ref[j * TOK : (j + 1) * TOK, :].T[HP:]
        cum = cum_ref[j : j + 1, :]
        c_cols = own_ref[j, 0, 4 * HD + NSTATE : 4 * HD + 2 * NSTATE]
        carried = jnp.dot(state, c_cols, preferred_element_type=F32)
        gated = (y_ref[j] + jnp.exp(cum + before) * carried) * (gate / (1.0 + jnp.exp(-gate)))
        mean = jnp.mean(gated * gated, axis=0, keepdims=True)
        out_ref[j] = (gated * lax.rsqrt(mean + 1e-05)).astype(BF16)
        before = before + cum[:, TOK - 1 : TOK]


def whole(array):
    return pl.BlockSpec(array.shape, lambda i, place: (0,) * array.ndim)


def of_core(gathered):
    return pl.BlockSpec((RING, 1) + gathered.shape[2:], lambda i, place: (0, place[1], 0, 0))


def on_core(kernel, place, gathered, before, after_own, out_shape):
    smem = pl.BlockSpec(memory_space=pltpu.SMEM)
    many = isinstance(out_shape, tuple)
    return pl.pallas_call(
        kernel,
        grid_spec=pltpu.PrefetchScalarGridSpec(
            num_scalar_prefetch=1,
            grid=(1,),
            in_specs=[whole(a) for a in before]
            + [of_core(gathered)]
            + [whole(a) if a.ndim > 1 else smem for a in after_own],
            out_specs=tuple(whole(o) for o in out_shape) if many else whole(out_shape),
        ),
        out_shape=out_shape,
        compiler_params=pltpu.CompilerParams(vmem_limit_bytes=VMEM_LIMIT),
    )(place, *before, gathered, *after_own)


def attention_kernel(place_ref, query_ref, gathered_ref, out_ref):
    group = query_ref.shape[0] // HD
    query = jnp.concatenate([query_ref[g * HD : (g + 1) * HD] for g in range(group)], axis=1)
    wide = group * TOK
    chunk = 4 * TOK
    query_start = place_ref[2]
    query_pos = query_start + lax.broadcasted_iota(jnp.int32, (1, wide), 1) % TOK

    def one(n, carry):
        other = n // 4
        core = (n // 2) % 2
        quad = n % 2
        start = place_ref[3 + other] + core * (RING * TOK) + quad * chunk

        def work(carry):
            best, total, summed = carry
            rows = pl.multiple_of(other * 2 * HD, 2 * HD)
            blocks = [(4 * quad + i, core) for i in range(4)]
            keys = jnp.concatenate([gathered_ref[z, k, pl.ds(rows, HD), :] for z, k in blocks], axis=0)
            values = jnp.concatenate([gathered_ref[z, k, pl.ds(rows + HD, HD), :] for z, k in blocks], axis=1)
            scores = jnp.dot(keys, query, preferred_element_type=F32) * HD ** (-0.5)
            key_pos = start + lax.broadcasted_iota(jnp.int32, (chunk, 1), 0)
            scores = jnp.where(key_pos <= query_pos, scores, -1e30)
            new_best = jnp.maximum(best, jnp.max(scores, axis=0, keepdims=True))
            fade = jnp.exp(best - new_best)
            weights = jnp.exp(scores - new_best).astype(BF16)
            total = total * fade + jnp.sum(weights.astype(F32), axis=0, keepdims=True)
            summed = summed * fade + jnp.dot(values, weights, preferred_element_type=F32)
            return new_best, total, summed

        return lax.cond(start < query_start + TOK, work, lambda c: c, carry)

    start = (jnp.full((1, wide), -1e30, F32), jnp.zeros((1, wide), F32), jnp.zeros((HD, wide), F32))
    _, total, summed = lax.fori_loop(0, 8, one, start)
    output = (summed / total).astype(BF16)
    for g in range(group):
        out_ref[g * HD : (g + 1) * HD] = output[:, g * TOK : (g + 1) * TOK]


def attention(place, query, gathered):
    return pl.pallas_call(
        attention_kernel,
        grid_spec=pltpu.PrefetchScalarGridSpec(
            num_scalar_prefetch=1,
            grid=(1,),
            in_specs=[whole(query), whole(gathered)],
            out_specs=whole(query),
        ),
        out_shape=jax.ShapeDtypeStruct(query.shape, BF16),
        compiler_params=pltpu.CompilerParams(vmem_limit_bytes=VMEM_LIMIT),
    )(place, query, gathered)


def heads_kernel(inputs_ref, gate_ref, out_ref):
    for h in range(inputs_ref.shape[1] // HP):
        columns = slice(h * HP, (h + 1) * HP)
        both = jnp.concatenate([inputs_ref[:, columns], gate_ref[:, columns]], axis=1)
        out_ref[:, 2 * h * HP : 2 * (h + 1) * HP] = both


def heads_together(w_inputs, w_gate):
    features, width = w_inputs.shape
    return pl.pallas_call(
        heads_kernel, out_shape=jax.ShapeDtypeStruct((features, 2 * width), BF16)
    )(w_inputs, w_gate)


def output_kernel(attn_ref, ssm_ref, w_attn_ref, w_ssm_ref, out_ref):
    attn = jnp.concatenate([attn_ref[0, 0], attn_ref[1, 0]], axis=1)
    ssm = jnp.concatenate([ssm_ref[:, 0, i].reshape(RING * HP, TOK) for i in range(2)], axis=1)
    total = jnp.dot(w_attn_ref[...], attn, preferred_element_type=F32)
    total = total + jnp.dot(w_ssm_ref[...], ssm, preferred_element_type=F32)
    half = total.shape[0] // 2
    out_ref[0] = jnp.concatenate([total[:half], total[half:]], axis=1).astype(BF16)


def output_terms(gathered, w_attn, w_ssm):
    width, attn_rows = w_attn.shape
    groups = gathered.shape[2] // HP
    by_head = gathered.reshape(RING, 2, groups, HP, TOK)
    first = attn_rows // HP // 2
    return pl.pallas_call(
        output_kernel,
        grid=(COLS,),
        in_specs=[
            pl.BlockSpec((2, 1, attn_rows, TOK), lambda b: (b % 4, b // 4, 0, 0)),
            pl.BlockSpec((RING, 1, 2, HP, TOK), lambda b: (0, b // 4, first + b % 4, 0, 0)),
            pl.BlockSpec((width, attn_rows), lambda b: (0, 0)),
            pl.BlockSpec((width, w_ssm.shape[1]), lambda b: (0, 0)),
        ],
        out_specs=pl.BlockSpec((1, width // 2, 4 * TOK), lambda b: (b, 0, 0)),
        out_shape=jax.ShapeDtypeStruct((COLS, width // 2, 4 * TOK), BF16),
        compiler_params=pltpu.CompilerParams(vmem_limit_bytes=VMEM_LIMIT),
    )(gathered, by_head, w_attn, w_ssm)


def on_device(
    hidden,
    w_query,
    w_key,
    w_value,
    w_ssm_in,
    w_gate,
    w_bc,
    w_dt,
    dt_bias,
    a_rate,
    d_skip,
    w_attn_out,
    w_ssm_out,
):
    row = lax.axis_index("row")
    seq = lax.axis_index("seq")
    chip = row // 2
    core = row % 2
    half_rows = hidden.shape[0]
    core_rows = half_rows // 2
    features = hidden.shape[1]
    heads = w_dt.shape[1]
    kv_width = w_value.shape[1]
    bc_width = w_bc.shape[1]

    kept = lax.dynamic_slice_in_dim(hidden, core * core_rows, core_rows, 0)
    sent = lax.dynamic_slice_in_dim(hidden, (1 - core) * core_rows, core_rows, 0)
    tokens = jnp.concatenate([kept, other_core(sent)], axis=1)

    def both_cores(own, axis):
        return jnp.concatenate([own, other_core(own)], axis=axis)

    def terms_of(product):
        def term(hop, *earlier):
            to_chip = (chip + hop + RING) % RING
            if earlier:
                to_chip = after(to_chip, *earlier)
            return lax.dynamic_slice_in_dim(product, to_chip * TOK, TOK, 1)

        return term

    w_first = both_cores(jnp.concatenate([w_key, w_value, w_bc, w_dt], axis=1), 0)
    first = Reduce(terms_of(by_rows(w_first, tokens)), F32, 4)
    first.hop(4)

    w_heads = both_cores(heads_together(after(w_ssm_in, *first.sent), w_gate), 0)
    third_product = jnp.dot(tokens, w_heads, preferred_element_type=F32)
    first.hop(3, *first.sent)
    w_second = both_cores(after(w_query, *first.sent), 0)
    second_product = by_rows(w_second, tokens)
    first.hop(2, *first.sent, third_product)
    first.hop(1, *first.sent, second_product)
    second = Reduce(terms_of(second_product), F32, 4)
    third = Reduce(terms_of(third_product), BF16, 3)
    second.hop(4, *first.sent)
    third.hop(4, *first.sent)
    kvbd = first.result()
    for hop in (3, 2, 1):
        third.hop(hop, *second.sent, *third.sent)
        second.hop(hop, *second.sent, *third.sent)
    ug = third.result()
    query = second.result().astype(BF16)

    key = kvbd[:kv_width].T.astype(BF16)
    value = kvbd[kv_width : 2 * kv_width].astype(BF16)
    bc_act = jax.nn.silu(kvbd[2 * kv_width : 2 * kv_width + bc_width]).astype(BF16)
    step_size = jax.nn.softplus(kvbd[2 * kv_width + bc_width :] + dt_bias[:, None])
    pair = jnp.concatenate([key, value], axis=0)
    pair_other = lax.ppermute(pair, "seq", [(0, 1), (1, 0)])
    step_high = step_size.astype(BF16)
    step_low = (step_size - step_high.astype(F32)).astype(BF16)
    message = jnp.concatenate([pair, pair_other, bc_act, step_high, step_low], axis=0)
    gathered = lax.all_gather(message, "row", axis=0, tiled=False).reshape((RING, 2) + message.shape)

    own_start = seq * half_rows
    place = jnp.stack(
        [
            chip,
            core,
            own_start + core * core_rows + chip * TOK,
            own_start,
            jnp.where(seq == 0, 1 << 20, 0),
        ]
    ).astype(jnp.int32)
    y, final, cum = on_core(
        scan_kernel,
        place,
        gathered,
        (ug,),
        (a_rate, d_skip),
        (
            jax.ShapeDtypeStruct((RING, HP, TOK), F32),
            jax.ShapeDtypeStruct((HP + 8, NSTATE), F32),
            jax.ShapeDtypeStruct((RING, TOK), F32),
        ),
    )
    theirs = other_core(final)
    early = jnp.where(core == 0, final, theirs)
    late = jnp.where(core == 0, theirs, final)
    half_end = jnp.exp(late[HP : HP + 1]) * early[:HP] + late[:HP]
    carried = jnp.where(seq == 0, 0.0, lax.ppermute(half_end, "seq", [(0, 1), (1, 0)]))
    prior = jnp.where(core == 0, carried, early[:HP] + jnp.exp(early[HP : HP + 1]) * carried)
    attn_out = attention(place, query, gathered)
    ssm_out = on_core(
        finish_kernel, place, gathered, (ug,), (cum, y, prior), jax.ShapeDtypeStruct((RING, HP, TOK), BF16)
    )

    mixer = jnp.concatenate([attn_out, ssm_out.reshape(RING * HP, TOK)], axis=0)
    mixers = lax.all_gather(mixer, "row", axis=0, tiled=False).reshape((RING, 2) + mixer.shape)
    terms = output_terms(mixers, w_attn_out.T, w_ssm_out.T)
    swapped = lax.all_to_all(terms, "col", 0, 0, tiled=True)
    mixed = jnp.sum(swapped.astype(F32), axis=0).astype(BF16)
    return jnp.concatenate([mixed[:, : 2 * TOK].T, mixed[:, 2 * TOK :].T], axis=1)


def solution(mesh):
    in_specs = (
        P("seq", "row"),
        P("row", "col"),
        P("row", "col"),
        P("row", "col"),
        P("row", "col"),
        P("row", "col"),
        P("row", None),
        P("row", "col"),
        P("col"),
        P("col"),
        P("col"),
        P("col", "row"),
        P("col", "row"),
    )
    out_specs = P(("seq", "col"), "row")
    return jax.shard_map(
        on_device, mesh=mesh, in_specs=in_specs, out_specs=out_specs, check_vma=False
    )
```

time: 240 us -> 224 us (0.933)
  waiting for transfers between devices: 114 us -> 87 us
  matrix products: 30.5 us -> 11.2 us
  starting transfers between devices: 29.4 us -> 47.2 us
  Pallas kernels: 0 us -> 12.3 us
  other arithmetic: 12.2 us -> 15.8 us
  local copies, waits for them, and re-layouts: 14.3 us -> 11.4 us
    all_gather x2, waiting for transfers between devices: 79.8 us -> 43.4 us  [the longest x1 43.4 us: on_device(): lax.all_gather(mixer, 'row', axis=0, tiled=False)]
    dot_general x24 -> x3, matrix products: 30.5 us -> 11.2 us  [the longest x2 5.89 us: by_rows(): lax.dot_general(weight, tokens, (((0,), (1,)), ((), ())), preferred_eleme...]
    pallas_call x0 -> x5, Pallas kernels: none -> 12.3 us  [the longest x2 3.67 us: on_core(): pl.pallas_call(kernel, grid_spec=pltpu.PrefetchScalarGridSpec(num_scalar_...]
    ppermute x3 -> x5, starting transfers between devices: 3.84 us -> 12.8 us  [other_core(): return lax.ppermute(array, 'row', [(i, i ^ 1) for i in range(ROWS)])]
    ppermute x14 -> x21, starting transfers between devices: 20.9 us -> 28.5 us  [ring_step(): lax.ppermute(array, 'row', [(i, (i + 2 * step) % ROWS) for i in range(ROW...]
    reduce_sum x6 -> x1, other arithmetic: 7.43 us -> 0.19 us  [on_device(): mixed = jnp.sum(swapped.astype(F32), axis=0).astype(BF16)]
    add x9 -> x6, other arithmetic: 0.44 us -> 6.73 us  [the longest x4 5.52 us: hop(): term = self.held[way].astype(F32) + term]
    convert_element_type x3 -> x4, other arithmetic: 0.05 us -> 6.24 us  [the longest x3 6.18 us: hop(): now[way] = term.astype(self.wire)]
  transfers between devices with their start and end apart: 21 -> 30, of which waited for: 9 -> 14; matrix products, arithmetic and copies ran while one was open for 15% -> 11% of each run, Pallas kernels for 0% -> 3%
where the time goes in v2:
time: 224 us
  waiting for transfers between devices  87 us (39%)
  starting transfers between devices  47.2 us (21%)
  blocking collectives  24.7 us (11%)
  other arithmetic  15.8 us (7%)
  between operations  13.8 us (6%)
  Pallas kernels  12.3 us (5%)
  local copies, waits for them, and re-layouts  11.4 us (5%)
  matrix products  11.2 us (5%)
    all_gather x1, waiting for transfers between devices, on_device(): lax.all_gather(mixer, 'row', axis=0, tiled=False)  43.4 us
    ppermute x21, waiting for transfers between devices, ring_step(): lax.ppermute(array, 'row', [(i, (i + 2 * step) % ROWS) for i in range(ROW...  38.5 us
    ppermute x21, starting transfers between devices, ring_step(): lax.ppermute(array, 'row', [(i, (i + 2 * step) % ROWS) for i in range(ROW...  28.5 us
    all_to_all x1, blocking collectives, on_device(): swapped = lax.all_to_all(terms, 'col', 0, 0, tiled=True)  24.7 us
    ppermute x5, starting transfers between devices, other_core(): return lax.ppermute(array, 'row', [(i, i ^ 1) for i in range(ROWS)])  12.8 us
    unnamed x35, local copies, waits for them, and re-layouts  6.58 us
    convert_element_type x3, other arithmetic, hop(): now[way] = term.astype(self.wire)  6.18 us
    dot_general x2, matrix products, by_rows(): lax.dot_general(weight, tokens, (((0,), (1,)), ((), ())), preferred_eleme...  5.89 us
  transfers between devices with their start and end apart: 30, of which 14 were waited for; matrix products, arithmetic and copies ran while one was open for 11% of the time, Pallas kernels for 3%

profile of v2, /device:TPU:1, one launch (start us, length us, event | category | flops | bytes accessed | tf_op | source)
XLA Modules:
  0.0 223.6 jit_solution(2979063980453860676)
XLA Ops:
  8.1 3.3 %collective-permute-start.1 = (bf16[1024,320]{0,1:T(8,128)(2,1)S(1)}, bf16[1024,320]{0,1:T(8,128)(2,1)S(1)}, u32[]{:S(2)}, u32[]{:S(2)}) collective-permute-start(bf16[1024,320]{0,1:T(8,128)(2,1)S(1)} %get-tuple-element.74), channel_id=1, source_target_pairs={{0,8},{8,0},{16,24},{24,16},{32,40},{40,32},{48,56},{56,48},{64,72... | collective-permute-start | bytes 1966088 | tf_op jit(solution)/shard_map/ppermute | solution.py:26
  11.8 2.0 collective-permute-done
  15.3 2.2 fusion.4
  17.6 2.2 shard_map.127
  20.2 10.5 %collective-permute-done.2 = f32[520,128]{1,0:T(8,128)S(1)} collective-permute-done((f32[520,128]{1,0:T(8,128)S(1)}, f32[520,128]{1,0:T(8,128)S(1)}, u32[]{:S(2)}, u32[]{:S(2)}) %collective-permute-start.2) | collective-permute-done | bytes 266272 | tf_op jit(solution)/shard_map/ppermute | solution.py:22
  31.4 2.7 %collective-permute-start.7 = (f32[520,128]{1,0:T(8,128)S(1)}, f32[520,128]{1,0:T(8,128)}, u32[]{:S(2)}, u32[]{:S(2)}) collective-permute-start(f32[520,128]{1,0:T(8,128)S(1)} %get-tuple-element.65), channel_id=1, source_target_pairs={{0,112},{8,120},{16,0},{24,8},{32,16},{40,24},{48,32},{56,40},{64,... | collective-permute-start | bytes 798728 | tf_op jit(solution)/shard_map/ppermute | solution.py:22
  35.4 5.3 %fusion = f32[1024,1024]{1,0:T(8,128)} fusion(bf16[320,1024]{1,0:T(8,128)(2,1)} %collective-permute-done.5, bf16[320,1024]{1,0:T(8,128)(2,1)} %shard_map.127, bf16[1024,320]{0,1:T(8,128)(2,1)} %copy-done.14, bf16[1024,320]{0,1:T(8,128)(2,1)S(1)} %get-tuple-element.73), kind=kOutput, calls=%fused_computation.1 | convolution fusion | flops 1347420160 | bytes 6815744 | tf_op jit(solution)/shard_map/dot_general | solution.py:294
  42.5 2.7 %collective-permute-start.8 = (f32[520,128]{1,0:T(8,128)S(1)}, f32[520,128]{1,0:T(8,128)}, u32[]{:S(2)}, u32[]{:S(2)}) collective-permute-start(f32[520,128]{1,0:T(8,128)S(1)} %get-tuple-element.63), channel_id=1, source_target_pairs={{0,112},{8,120},{16,0},{24,8},{32,16},{40,24},{48,32},{56,40},{64,... | collective-permute-start | bytes 798728 | tf_op jit(solution)/shard_map/ppermute | solution.py:22
  45.1 3.7 %fusion.14 = f32[512,1024]{1,0:T(8,128)} fusion(bf16[320,512]{1,0:T(8,128)(2,1)} %collective-permute-done.3, bf16[320,512]{1,0:T(8,128)(2,1)} %param.14, bf16[1024,320]{0,1:T(8,128)(2,1)} %copy-done.14, bf16[1024,320]{0,1:T(8,128)(2,1)S(1)} %get-tuple-element.73), kind=kOutput, calls=%fused_computation.15 | convolution fusion | flops 675020800 | bytes 4063232 | tf_op jit(solution)/shard_map/dot_general | solution.py:59
  48.8 2.0 collective-permute-done.6
  52.6 2.7 %collective-permute-start.22 = (f32[520,128]{1,0:T(8,128)S(1)}, f32[520,128]{1,0:T(8,128)S(1)}, u32[]{:S(2)}, u32[]{:S(2)}) collective-permute-start(f32[520,128]{1,0:T(8,128)S(1)} %get-tuple-element.61), channel_id=1, source_target_pairs={{0,112},{8,120},{16,0},{24,8},{32,16},{40,24},{48,32},{56,40},{64,... | collective-permute-start | bytes 798728 | tf_op jit(solution)/shard_map/ppermute | solution.py:22
  55.3 4.8 %collective-permute-done.21 = f32[520,128]{1,0:T(8,128)S(1)} collective-permute-done((f32[520,128]{1,0:T(8,128)}, f32[520,128]{1,0:T(8,128)S(1)}, u32[]{:S(2)}, u32[]{:S(2)}) %collective-permute-start.21) | collective-permute-done | bytes 266272 | tf_op jit(solution)/shard_map/ppermute | solution.py:22
  65.8 2.3 %collective-permute-start.10 = (bf16[1024,128]{1,0:T(8,128)(2,1)S(1)}, bf16[1024,128]{1,0:T(8,128)(2,1)S(1)}, u32[]{:S(2)}, u32[]{:S(2)}) collective-permute-start(bf16[1024,128]{1,0:T(8,128)(2,1)S(1)} %dynamic-slice_convert_fusion.1), channel_id=1, source_target_pairs={{0,112},{8,120},{16,0},{24,8},{32,16},{40,24},{48,32},{56,40},{64,... | collective-permute-start | bytes 786440 | tf_op jit(solution)/shard_map/ppermute | solution.py:22
  73.2 3.1 %collective-permute-start.13 = (bf16[1024,128]{1,0:T(8,128)(2,1)}, bf16[1024,128]{1,0:T(8,128)(2,1)}, u32[]{:S(2)}, u32[]{:S(2)}) collective-permute-start(bf16[1024,128]{1,0:T(8,128)(2,1)} %add_convert_fusion.4), channel_id=1, source_target_pairs={{0,112},{8,120},{16,0},{24,8},{32,16},{40,24},{48,32},{56,40},{64,... | collective-permute-start | bytes 786440 | tf_op jit(solution)/shard_map/ppermute | solution.py:22
  76.5 2.7 %collective-permute-start.15 = (f32[512,128]{1,0:T(8,128)S(1)}, f32[512,128]{1,0:T(8,128)S(1)}, u32[]{:S(2)}, u32[]{:S(2)}) collective-permute-start(f32[512,128]{1,0:T(8,128)S(1)} %get-tuple-element.71), channel_id=1, source_target_pairs={{0,112},{8,120},{16,0},{24,8},{32,16},{40,24},{48,32},{56,40},{64,... | collective-permute-start | bytes 786440 | tf_op jit(solution)/shard_map/ppermute | solution.py:22
  80.1 2.2 add_convert_fusion.2
  85.4 3.1 %collective-permute-done.11 = f32[512,128]{1,0:T(8,128)S(1)} collective-permute-done((f32[512,128]{1,0:T(8,128)S(1)}, f32[512,128]{1,0:T(8,128)S(1)}, u32[]{:S(2)}, u32[]{:S(2)}) %collective-permute-start.11) | collective-permute-done | bytes 262176 | tf_op jit(solution)/shard_map/ppermute | solution.py:22
  88.8 2.5 %collective-permute-start.19 = (f32[512,128]{1,0:T(8,128)S(1)}, f32[512,128]{1,0:T(8,128)}, u32[]{:S(2)}, u32[]{:S(2)}) collective-permute-start(f32[512,128]{1,0:T(8,128)S(1)} %get-tuple-element.69), channel_id=1, source_target_pairs={{0,112},{8,120},{16,0},{24,8},{32,16},{40,24},{48,32},{56,40},{64,... | collective-permute-start | bytes 786440 | tf_op jit(solution)/shard_map/ppermute | solution.py:22
  91.4 8.4 %collective-permute-done.16 = bf16[1024,128]{1,0:T(8,128)(2,1)} collective-permute-done((bf16[1024,128]{1,0:T(8,128)(2,1)}, bf16[1024,128]{1,0:T(8,128)(2,1)}, u32[]{:S(2)}, u32[]{:S(2)}) %collective-permute-start.16) | collective-permute-done | bytes 262176 | tf_op jit(solution)/shard_map/ppermute | solution.py:22
  99.7 2.2 add_convert_fusion.1
  101.9 2.7 %collective-permute-start.25 = (bf16[1024,128]{1,0:T(8,128)(2,1)S(1)}, bf16[1024,128]{1,0:T(8,128)(2,1)}, u32[]{:S(2)}, u32[]{:S(2)}) collective-permute-start(bf16[1024,128]{1,0:T(8,128)(2,1)S(1)} %get-tuple-element.58), channel_id=1, source_target_pairs={{0,112},{8,120},{16,0},{24,8},{32,16},{40,24},{48,32},{56,40},{64,... | collective-permute-start | bytes 786440 | tf_op jit(solution)/shard_map/ppermute | solution.py:22
  104.6 6.4 %collective-permute-done.14 = f32[512,128]{1,0:T(8,128)S(1)} collective-permute-done((f32[512,128]{1,0:T(8,128)S(1)}, f32[512,128]{1,0:T(8,128)S(1)}, u32[]{:S(2)}, u32[]{:S(2)}) %collective-permute-start.14) | collective-permute-done | bytes 262176 | tf_op jit(solution)/shard_map/ppermute | solution.py:22
  112.9 2.7 %collective-permute-start.20 = (f32[512,128]{1,0:T(8,128)}, f32[512,128]{1,0:T(8,128)S(1)}, u32[]{:S(2)}, u32[]{:S(2)}) collective-permute-start(f32[512,128]{1,0:T(8,128)} %get-tuple-element.68), channel_id=1, source_target_pairs={{0,112},{8,120},{16,0},{24,8},{32,16},{40,24},{48,32},{56,40},{64,... | collective-permute-start | bytes 786440 | tf_op jit(solution)/shard_map/ppermute | solution.py:22
  115.6 2.4 %collective-permute-done.24 = bf16[1024,128]{1,0:T(8,128)(2,1)S(1)} collective-permute-done((bf16[1024,128]{1,0:T(8,128)(2,1)}, bf16[1024,128]{1,0:T(8,128)(2,1)S(1)}, u32[]{:S(2)}, u32[]{:S(2)}) %collective-permute-start.24) | collective-permute-done | bytes 262176 | tf_op jit(solution)/shard_map/ppermute | solution.py:22
  121.2 2.8 %shard_map.129 = (f32[8,64,128]{2,1,0:T(8,128)S(1)}, f32[72,128]{1,0:T(8,128)S(1)}, f32[8,128]{1,0:T(8,128)S(1)}) custom-call(s32[5]{0:T(128)S(1)} %stack.23.place_ref, f32[1024,128]{1,0:T(8,128)S(1)} %convert_add_fusion.ug_ref, bf16[8,2,784,128]{3,2,1,0:T(8,128)(2,1)S(1)} %bitcast.21, f32[8]{0:T(128)S(1)} %copy-done.5, f32[8]{0:T(128)S(1)} %copy-done.6), custom_call_target="tpu_custom_call" | custom-call | tf_op jit(solution)/shard_map/pallas_call | solution.py:136
  124.0 7.7 %collective-permute-start.26 = (f32[72,128]{1,0:T(8,128)S(1)}, f32[72,128]{1,0:T(8,128)S(1)}, u32[]{:S(2)}, u32[]{:S(2)}) collective-permute-start(f32[72,128]{1,0:T(8,128)S(1)} %get-tuple-element.54), channel_id=1, source_target_pairs={{0,8},{8,0},{16,24},{24,16},{32,40},{40,32},{48,56},{56,48},{64,72... | collective-permute-start | bytes 110600 | tf_op jit(solution)/shard_map/ppermute | solution.py:26
  131.8 3.2 %shard_map.128 = bf16[512,128]{1,0:T(8,128)(2,1)S(1)} custom-call(s32[5]{0:T(128)S(1)} %stack.23.place_ref, bf16[512,128]{1,0:T(8,128)(2,1)S(1)} %add_convert_fusion.5.query_ref, bf16[8,2,784,128]{3,2,1,0:T(8,128)(2,1)S(1)} %bitcast.22), custom_call_target="tpu_custom_call" | custom-call | tf_op jit(solution)/shard_map/pallas_call | solution.py:191
  135.1 4.3 %collective-permute-start.27 = (f32[64,128]{1,0:T(8,128)S(1)}, f32[64,128]{1,0:T(8,128)S(1)}, u32[]{:S(2)}, u32[]{:S(2)}) collective-permute-start(f32[64,128]{1,0:T(8,128)S(1)} %slice_add_fusion), channel_id=1, source_target_pairs={{0,128},{128,0},{1,129},{129,1},{2,130},{130,2},{3,131},{131,3},{4... | collective-permute-start | bytes 98312 | tf_op jit(solution)/shard_map/ppermute | solution.py:348
  142.3 43.4 %all-gather.7.cloned.1.call-done = bf16[16384,128]{1,0:T(8,128)(2,1)} async-done(((bf16[1024,128]{1,0:T(8,128)(2,1)}), bf16[16384,128]{1,0:T(8,128)(2,1)}) %all-gather.7.cloned.1.call-update) | async-done | bytes 4194320 | tf_op jit(solution)/shard_map/all_gather | solution.py:356
  185.7 2.2 copy-done.2
  187.9 3.2 %shard_map.131 = bf16[8,160,512]{2,1,0:T(8,128)(2,1)S(1)} custom-call(bf16[8,2,1024,128]{3,2,1,0:T(8,128)(2,1)S(1)} %bitcast.24, bf16[8,2,16,64,128]{4,3,2,1,0:T(8,128)(2,1)S(1)} %bitcast.25, bf16[320,512]{1,0:T(8,128)(2,1)S(1)} %bitcast.27, bf16[320,512]{1,0:T(8,128)(2,1)S(1)} %bitcast.28), custom_call_target="tpu_custom_call" | custom-call | tf_op jit(solution)/shard_map/pallas_call | solution.py:232
  191.2 24.7 %all_to_all.5 = bf16[8,160,512]{2,1,0:T(8,128)(2,1)S(1)} all-to-all(bf16[8,160,512]{2,1,0:T(8,128)(2,1)S(1)} %shard_map.131), channel_id=1, replica_groups=mesh['seq'=2,'row'=16,'col'=8] {'col'}, dimensions={0} | all-to-all | bytes 2621440 | tf_op jit(solution)/shard_map/all_to_all | solution.py:358
  (109 shorter events, 33.8 us)
Async XLA Ops:
  6.5 112.7 %all-gather.5.cloned.1.call-start = ((), (), s32[]{:S(2)}) async-start(), calls=%async_computation.1 | async-start | bytes 3411968 | tf_op jit(solution)/shard_map/all_gather | solution.py:320
  8.1 5.6 %collective-permute-start.1 = (bf16[1024,320]{0,1:T(8,128)(2,1)S(1)}, bf16[1024,320]{0,1:T(8,128)(2,1)S(1)}, u32[]{:S(2)}, u32[]{:S(2)}) collective-permute-start(bf16[1024,320]{0,1:T(8,128)(2,1)S(1)} %get-tuple-element.74), channel_id=1, source_target_pairs={{0,8},{8,0},{16,24},{24,16},{32,40},{40,32},{48,56},{56,48},{64,72... | collective-permute-start | bytes 1966088 | tf_op jit(solution)/shard_map/ppermute | solution.py:26
  11.6 2.1 collective-permute-start
  19.8 15.6 %collective-permute-start.5 = (bf16[320,1024]{1,0:T(8,128)(2,1)}, bf16[320,1024]{1,0:T(8,128)(2,1)}, u32[]{:S(2)}, u32[]{:S(2)}) collective-permute-start(bf16[320,1024]{1,0:T(8,128)(2,1)} %shard_map.127), channel_id=1, source_target_pairs={{0,8},{8,0},{16,24},{24,16},{32,40},{40,32},{48,56},{56,48},{64,72... | collective-permute-start | bytes 1966088 | tf_op jit(solution)/shard_map/ppermute | solution.py:26
  20.2 10.5 %collective-permute-start.2 = (f32[520,128]{1,0:T(8,128)S(1)}, f32[520,128]{1,0:T(8,128)S(1)}, u32[]{:S(2)}, u32[]{:S(2)}) collective-permute-start(f32[520,128]{1,0:T(8,128)S(1)} %constant_dynamic-slice_fusion.3), channel_id=1, source_target_pairs={{0,16},{8,24},{16,32},{24,40},{32,48},{40,56},{48,64},{56,72},{64,... | collective-permute-start | bytes 798728 | tf_op jit(solution)/shard_map/ppermute | solution.py:22
  31.4 9.3 %collective-permute-start.4 = (f32[520,128]{1,0:T(8,128)}, f32[520,128]{1,0:T(8,128)S(1)}, u32[]{:S(2)}, u32[]{:S(2)}) collective-permute-start(f32[520,128]{1,0:T(8,128)} %get-tuple-element.66), channel_id=1, source_target_pairs={{0,16},{8,24},{16,32},{24,40},{32,48},{40,56},{48,64},{56,72},{64,... | collective-permute-start | bytes 798728 | tf_op jit(solution)/shard_map/ppermute | solution.py:22
  31.4 9.3 %collective-permute-start.7 = (f32[520,128]{1,0:T(8,128)S(1)}, f32[520,128]{1,0:T(8,128)}, u32[]{:S(2)}, u32[]{:S(2)}) collective-permute-start(f32[520,128]{1,0:T(8,128)S(1)} %get-tuple-element.65), channel_id=1, source_target_pairs={{0,112},{8,120},{16,0},{24,8},{32,16},{40,24},{48,32},{56,40},{64,... | collective-permute-start | bytes 798728 | tf_op jit(solution)/shard_map/ppermute | solution.py:22
  34.1 11.0 %collective-permute-start.3 = (bf16[320,512]{1,0:T(8,128)(2,1)}, bf16[320,512]{1,0:T(8,128)(2,1)}, u32[]{:S(2)}, u32[]{:S(2)}) collective-permute-start(bf16[320,512]{1,0:T(8,128)(2,1)} %param.14), channel_id=1, source_target_pairs={{0,8},{8,0},{16,24},{24,16},{32,40},{40,32},{48,56},{56,48},{64,72... | collective-permute-start | bytes 983048 | tf_op jit(solution)/shard_map/ppermute | solution.py:26
  42.5 8.4 %collective-permute-start.6 = (f32[520,128]{1,0:T(8,128)}, f32[520,128]{1,0:T(8,128)S(1)}, u32[]{:S(2)}, u32[]{:S(2)}) collective-permute-start(f32[520,128]{1,0:T(8,128)} %get-tuple-element.64), channel_id=1, source_target_pairs={{0,16},{8,24},{16,32},{24,40},{32,48},{40,56},{48,64},{56,72},{64,... | collective-permute-start | bytes 798728 | tf_op jit(solution)/shard_map/ppermute | solution.py:22
  42.5 8.4 %collective-permute-start.8 = (f32[520,128]{1,0:T(8,128)S(1)}, f32[520,128]{1,0:T(8,128)}, u32[]{:S(2)}, u32[]{:S(2)}) collective-permute-start(f32[520,128]{1,0:T(8,128)S(1)} %get-tuple-element.63), channel_id=1, source_target_pairs={{0,112},{8,120},{16,0},{24,8},{32,16},{40,24},{48,32},{56,40},{64,... | collective-permute-start | bytes 798728 | tf_op jit(solution)/shard_map/ppermute | solution.py:22
  52.6 7.4 %collective-permute-start.21 = (f32[520,128]{1,0:T(8,128)}, f32[520,128]{1,0:T(8,128)S(1)}, u32[]{:S(2)}, u32[]{:S(2)}) collective-permute-start(f32[520,128]{1,0:T(8,128)} %get-tuple-element.62), channel_id=1, source_target_pairs={{0,16},{8,24},{16,32},{24,40},{32,48},{40,56},{48,64},{56,72},{64,... | collective-permute-start | bytes 798728 | tf_op jit(solution)/shard_map/ppermute | solution.py:22
  52.6 7.4 %collective-permute-start.22 = (f32[520,128]{1,0:T(8,128)S(1)}, f32[520,128]{1,0:T(8,128)S(1)}, u32[]{:S(2)}, u32[]{:S(2)}) collective-permute-start(f32[520,128]{1,0:T(8,128)S(1)} %get-tuple-element.61), channel_id=1, source_target_pairs={{0,112},{8,120},{16,0},{24,8},{32,16},{40,24},{48,32},{56,40},{64,... | collective-permute-start | bytes 798728 | tf_op jit(solution)/shard_map/ppermute | solution.py:22
  60.3 3.4 %collective-permute-start.23 = (bf16[256,128]{1,0:T(8,128)(2,1)S(1)}, bf16[256,128]{1,0:T(8,128)(2,1)S(1)}, u32[]{:S(2)}, u32[]{:S(2)}) collective-permute-start(bf16[256,128]{1,0:T(8,128)(2,1)S(1)} %pad_maximum_fusion.7), channel_id=1, source_target_pairs={{0,128},{128,0},{1,129},{129,1},{2,130},{130,2},{3,131},{131,3},{4... | collective-permute-start | bytes 196616 | tf_op jit(solution)/shard_map/ppermute | solution.py:316
  64.7 121.1 %all-gather.7.cloned.1.call-start = ((), (), s32[]{:S(2)}) async-start(), calls=%async_computation.2 | async-start | bytes 4456448 | tf_op jit(solution)/shard_map/all_gather | solution.py:356
  65.8 5.6 %collective-permute-start.10 = (bf16[1024,128]{1,0:T(8,128)(2,1)S(1)}, bf16[1024,128]{1,0:T(8,128)(2,1)S(1)}, u32[]{:S(2)}, u32[]{:S(2)}) collective-permute-start(bf16[1024,128]{1,0:T(8,128)(2,1)S(1)} %dynamic-slice_convert_fusion.1), channel_id=1, source_target_pairs={{0,112},{8,120},{16,0},{24,8},{32,16},{40,24},{48,32},{56,40},{64,... | collective-permute-start | bytes 786440 | tf_op jit(solution)/shard_map/ppermute | solution.py:22
  69.0 7.3 %collective-permute-start.9 = (f32[512,128]{1,0:T(8,128)S(1)}, f32[512,128]{1,0:T(8,128)S(1)}, u32[]{:S(2)}, u32[]{:S(2)}) collective-permute-start(f32[512,128]{1,0:T(8,128)S(1)} %constant_dynamic-slice_fusion.1), channel_id=1, source_target_pairs={{0,16},{8,24},{16,32},{24,40},{32,48},{40,56},{48,64},{56,72},{64,... | collective-permute-start | bytes 786440 | tf_op jit(solution)/shard_map/ppermute | solution.py:22
  70.2 9.0 %collective-permute-start.12 = (bf16[1024,128]{1,0:T(8,128)(2,1)S(1)}, bf16[1024,128]{1,0:T(8,128)(2,1)}, u32[]{:S(2)}, u32[]{:S(2)}) collective-permute-start(bf16[1024,128]{1,0:T(8,128)(2,1)S(1)} %dynamic-slice_convert_fusion), channel_id=1, source_target_pairs={{0,16},{8,24},{16,32},{24,40},{32,48},{40,56},{48,64},{56,72},{64,... | collective-permute-start | bytes 786440 | tf_op jit(solution)/shard_map/ppermute | solution.py:22
  73.2 6.8 %collective-permute-start.13 = (bf16[1024,128]{1,0:T(8,128)(2,1)}, bf16[1024,128]{1,0:T(8,128)(2,1)}, u32[]{:S(2)}, u32[]{:S(2)}) collective-permute-start(bf16[1024,128]{1,0:T(8,128)(2,1)} %add_convert_fusion.4), channel_id=1, source_target_pairs={{0,112},{8,120},{16,0},{24,8},{32,16},{40,24},{48,32},{56,40},{64,... | collective-permute-start | bytes 786440 | tf_op jit(solution)/shard_map/ppermute | solution.py:22
  76.4 12.1 %collective-permute-start.11 = (f32[512,128]{1,0:T(8,128)S(1)}, f32[512,128]{1,0:T(8,128)S(1)}, u32[]{:S(2)}, u32[]{:S(2)}) collective-permute-start(f32[512,128]{1,0:T(8,128)S(1)} %get-tuple-element.72), channel_id=1, source_target_pairs={{0,16},{8,24},{16,32},{24,40},{32,48},{40,56},{48,64},{56,72},{64,... | collective-permute-start | bytes 786440 | tf_op jit(solution)/shard_map/ppermute | solution.py:22
  76.5 12.0 %collective-permute-start.15 = (f32[512,128]{1,0:T(8,128)S(1)}, f32[512,128]{1,0:T(8,128)S(1)}, u32[]{:S(2)}, u32[]{:S(2)}) collective-permute-start(f32[512,128]{1,0:T(8,128)S(1)} %get-tuple-element.71), channel_id=1, source_target_pairs={{0,112},{8,120},{16,0},{24,8},{32,16},{40,24},{48,32},{56,40},{64,... | collective-permute-start | bytes 786440 | tf_op jit(solution)/shard_map/ppermute | solution.py:22
  82.2 17.5 %collective-permute-start.16 = (bf16[1024,128]{1,0:T(8,128)(2,1)}, bf16[1024,128]{1,0:T(8,128)(2,1)}, u32[]{:S(2)}, u32[]{:S(2)}) collective-permute-start(bf16[1024,128]{1,0:T(8,128)(2,1)} %get-tuple-element.60), channel_id=1, source_target_pairs={{0,16},{8,24},{16,32},{24,40},{32,48},{40,56},{48,64},{56,72},{64,... | collective-permute-start | bytes 786440 | tf_op jit(solution)/shard_map/ppermute | solution.py:22
  84.0 15.7 %collective-permute-start.17 = (bf16[1024,128]{1,0:T(8,128)(2,1)S(1)}, bf16[1024,128]{1,0:T(8,128)(2,1)}, u32[]{:S(2)}, u32[]{:S(2)}) collective-permute-start(bf16[1024,128]{1,0:T(8,128)(2,1)S(1)} %get-tuple-element.59), channel_id=1, source_target_pairs={{0,112},{8,120},{16,0},{24,8},{32,16},{40,24},{48,32},{56,40},{64,... | collective-permute-start | bytes 786440 | tf_op jit(solution)/shard_map/ppermute | solution.py:22
  88.6 22.4 %collective-permute-start.14 = (f32[512,128]{1,0:T(8,128)S(1)}, f32[512,128]{1,0:T(8,128)S(1)}, u32[]{:S(2)}, u32[]{:S(2)}) collective-permute-start(f32[512,128]{1,0:T(8,128)S(1)} %get-tuple-element.70), channel_id=1, source_target_pairs={{0,16},{8,24},{16,32},{24,40},{32,48},{40,56},{48,64},{56,72},{64,... | collective-permute-start | bytes 786440 | tf_op jit(solution)/shard_map/ppermute | solution.py:22
  88.8 22.1 %collective-permute-start.19 = (f32[512,128]{1,0:T(8,128)S(1)}, f32[512,128]{1,0:T(8,128)}, u32[]{:S(2)}, u32[]{:S(2)}) collective-permute-start(f32[512,128]{1,0:T(8,128)S(1)} %get-tuple-element.69), channel_id=1, source_target_pairs={{0,112},{8,120},{16,0},{24,8},{32,16},{40,24},{48,32},{56,40},{64,... | collective-permute-start | bytes 786440 | tf_op jit(solution)/shard_map/ppermute | solution.py:22
  101.9 16.1 %collective-permute-start.24 = (bf16[1024,128]{1,0:T(8,128)(2,1)}, bf16[1024,128]{1,0:T(8,128)(2,1)S(1)}, u32[]{:S(2)}, u32[]{:S(2)}) collective-permute-start(bf16[1024,128]{1,0:T(8,128)(2,1)} %get-tuple-element.57), channel_id=1, source_target_pairs={{0,16},{8,24},{16,32},{24,40},{32,48},{40,56},{48,64},{56,72},{64,... | collective-permute-start | bytes 786440 | tf_op jit(solution)/shard_map/ppermute | solution.py:22
  101.9 16.1 %collective-permute-start.25 = (bf16[1024,128]{1,0:T(8,128)(2,1)S(1)}, bf16[1024,128]{1,0:T(8,128)(2,1)}, u32[]{:S(2)}, u32[]{:S(2)}) collective-permute-start(bf16[1024,128]{1,0:T(8,128)(2,1)S(1)} %get-tuple-element.58), channel_id=1, source_target_pairs={{0,112},{8,120},{16,0},{24,8},{32,16},{40,24},{48,32},{56,40},{64,... | collective-permute-start | bytes 786440 | tf_op jit(solution)/shard_map/ppermute | solution.py:22
  112.9 18.8 %collective-permute-start.18 = (f32[512,128]{1,0:T(8,128)}, f32[512,128]{1,0:T(8,128)S(1)}, u32[]{:S(2)}, u32[]{:S(2)}) collective-permute-start(f32[512,128]{1,0:T(8,128)} %get-tuple-element.67), channel_id=1, source_target_pairs={{0,16},{8,24},{16,32},{24,40},{32,48},{40,56},{48,64},{56,72},{64,... | collective-permute-start | bytes 786440 | tf_op jit(solution)/shard_map/ppermute | solution.py:22
  112.9 18.8 %collective-permute-start.20 = (f32[512,128]{1,0:T(8,128)}, f32[512,128]{1,0:T(8,128)S(1)}, u32[]{:S(2)}, u32[]{:S(2)}) collective-permute-start(f32[512,128]{1,0:T(8,128)} %get-tuple-element.68), channel_id=1, source_target_pairs={{0,112},{8,120},{16,0},{24,8},{32,16},{40,24},{48,32},{56,40},{64,... | collective-permute-start | bytes 786440 | tf_op jit(solution)/shard_map/ppermute | solution.py:22
  124.0 11.0 %collective-permute-start.26 = (f32[72,128]{1,0:T(8,128)S(1)}, f32[72,128]{1,0:T(8,128)S(1)}, u32[]{:S(2)}, u32[]{:S(2)}) collective-permute-start(f32[72,128]{1,0:T(8,128)S(1)} %get-tuple-element.54), channel_id=1, source_target_pairs={{0,8},{8,0},{16,24},{24,16},{32,40},{40,32},{48,56},{56,48},{64,72... | collective-permute-start | bytes 110600 | tf_op jit(solution)/shard_map/ppermute | solution.py:26
  135.1 5.6 %collective-permute-start.27 = (f32[64,128]{1,0:T(8,128)S(1)}, f32[64,128]{1,0:T(8,128)S(1)}, u32[]{:S(2)}, u32[]{:S(2)}) collective-permute-start(f32[64,128]{1,0:T(8,128)S(1)} %slice_add_fusion), channel_id=1, source_target_pairs={{0,128},{128,0},{1,129},{129,1},{2,130},{130,2},{3,131},{131,3},{4... | collective-permute-start | bytes 98312 | tf_op jit(solution)/shard_map/ppermute | solution.py:348
  140.7 45.0 %copy-start.3 = (bf16[512,320]{0,1:T(8,128)(2,1)S(1)}, bf16[512,320]{0,1:T(8,128)(2,1)}, u32[]{:S(2)}) copy-start(bf16[512,320]{0,1:T(8,128)(2,1)} %param.24) | copy-start | bytes 983044
  140.7 45.0 %copy-start.4 = (bf16[512,320]{0,1:T(8,128)(2,1)S(1)}, bf16[512,320]{0,1:T(8,128)(2,1)}, u32[]{:S(2)}) copy-start(bf16[512,320]{0,1:T(8,128)(2,1)} %param.25) | copy-start | bytes 983044
  (14 other events, 102.8 us)
Sparse Core Ops, SparseCore 0:
  64.8 50.8 all-gather.4
  142.4 43.2 all-gather.6
